TPU v7x, 32 devices: a whole 2x2x4 slice. The times are simulated.
32 devices in a mesh: dp: 8 (over z, y), bn: 4 (over x, core).
Axes of the slice: x: 2, y: 2, z: 4, core: 2. Of those that a mesh axis runs over, the one named last changes fastest.
Arguments:
- images: bfloat16 [32, 38, 38, 512], P(('dp', 'bn')), may hold values from -6 to 6
- image_count: int32 [32], P(('dp', 'bn')), may hold values from 0 to 1, as said below
- image_size: int32 [32], P(('dp', 'bn')), may hold values from 16 to 19, as said below
- cotangent: bfloat16 [32, 19, 19, 1024], P(('dp', 'bn')), may hold values from -6 to 6
- stem_weight: bfloat16 [512, 3, 3, 1024], replicated, may hold values from -0.09375 to 0.09375
- split_main: bfloat16 [1024, 512], replicated, may hold values from -0.1875 to 0.1875
- split_side: bfloat16 [1024, 512], replicated, may hold values from -0.1875 to 0.1875
- block_reduce: bfloat16 [512, 512], replicated, may hold values from -0.25 to 0.25
- block_spatial: bfloat16 [512, 3, 3, 512], replicated, may hold values from -0.09375 to 0.09375
- block_transit: bfloat16 [512, 512], replicated, may hold values from -0.25 to 0.25
- merge_weight: bfloat16 [1024, 1024], replicated, may hold values from -0.1875 to 0.1875
- affines: float32 [3072, 2], replicated, may hold values from -0.5 to 1.5
Outputs:
- activations: float32 [32, 19, 19, 1024], P(('dp', 'bn'))
- image_grad: float32 [32, 38, 38, 512], P(('dp', 'bn'))
- grad_stem: float32 [512, 3, 3, 1024], P('dp')
- grad_main: float32 [1024, 512], P('dp')
- grad_side: float32 [1024, 512], P('dp')
- grad_reduce: float32 [512, 512], P('dp')
- grad_spatial: float32 [512, 3, 3, 512], P('dp')
- grad_transit: float32 [512, 512], P('dp')
- grad_merge: float32 [1024, 1024], P('dp')
- affine_grad: float32 [3072, 2], P('dp')
Inputs may be any that keep to these rules, and one draw needn't show every extreme that they name: `image_count`: in each group of 4 devices that share a dp index, some device holds 1 images; other devices may hold none. A device's images fill its first slots. `image_size`: each slot's size is 16 or 19; an image of size s fills the first 2 s input rows and columns of its slot, and what lies outside is not read for any output.
All inputs are finite; a program needn't handle non-finite values.
Results may differ from a plain program's by a relative error of at most 0.015.
Values sent between devices are 32-bit elements; how exact they have to be, the bound alone decides.
A program may use at most 256 MiB of HBM per device.

v0:
```python
import jax
import jax.numpy as jnp
from jax import lax
from jax.sharding import PartitionSpec as P

EPS = 1e-05


def mish(value):
    return value * jnp.tanh(jax.nn.softplus(value))


def matmul(left, right):
    return jnp.dot(left, right, preferred_element_type=jnp.float32)


def outer_sum(left, right):
    return lax.dot_general(
        left, right, (((0,), (0,)), ((), ())), preferred_element_type=jnp.float32
    )


def against(left, right):
    return lax.dot_general(
        left, right, (((1,), (1,)), ((), ())), preferred_element_type=jnp.float32
    )


def stride_taps(field, grid):
    padded = jnp.pad(field, ((0, 0), (1, 1), (1, 1), (0, 0)))
    reach = 2 * grid - 1
    return [
        padded[:, a : a + reach : 2, b : b + reach : 2, :].reshape(-1, field.shape[3])
        for a in range(3)
        for b in range(3)
    ]


def unit_taps(field, grid):
    padded = jnp.pad(field, ((0, 0), (1, 1), (1, 1), (0, 0)))
    return [
        padded[:, a : a + grid, b : b + grid, :].reshape(-1, field.shape[3])
        for a in range(3)
        for b in range(3)
    ]


def apply_taps(taps, weight):
    return sum((matmul(tap, weight[:, k // 3, k % 3, :]) for k, tap in enumerate(taps)))


def taps_grad(taps, upstream, weight):
    stacked = jnp.stack([outer_sum(tap, upstream) for tap in taps], axis=1)
    return stacked.reshape(weight.shape)


def stride_back(upstream, weight, slots, grid):
    channels = weight.shape[0]
    result = jnp.zeros((slots, 2 * grid + 2, 2 * grid + 2, channels), jnp.float32)
    for a in range(3):
        for b in range(3):
            piece = against(upstream, weight[:, a, b, :]).reshape(slots, grid, grid, channels)
            result = result + lax.pad(
                piece, jnp.float32(0), ((0, 0, 0), (a, 3 - a, 1), (b, 3 - b, 1), (0, 0, 0))
            )
    return result[:, 1 : 2 * grid + 1, 1 : 2 * grid + 1, :]


def unit_back(upstream, weight, slots, grid):
    channels = weight.shape[0]
    result = jnp.zeros((slots, grid + 2, grid + 2, channels), jnp.float32)
    for a in range(3):
        for b in range(3):
            piece = against(upstream, weight[:, a, b, :]).reshape(slots, grid, grid, channels)
            result = result + lax.pad(
                piece, jnp.float32(0), ((0, 0, 0), (a, 2 - a, 0), (b, 2 - b, 0), (0, 0, 0))
            )
    return result[:, 1 : grid + 1, 1 : grid + 1, :].reshape(-1, channels)


def normalize(values, mask, local_count, gain, shift):
    total = jnp.sum(values * mask, axis=0)
    square = jnp.sum(values * values * mask, axis=0)
    total, square, count = lax.psum((total, square, local_count), "bn")
    mean = total / count
    spread = square / count - mean * mean
    inverse = lax.rsqrt(spread + EPS)
    scaled = (values - mean) * inverse
    before = scaled * gain + shift
    return (mish(before) * mask, (scaled, inverse, before, count))


def normalize_back(upstream, kept, mask, gain):
    scaled, inverse, before, count = kept
    unused, mish_back = jax.vjp(mish, before)
    inner = mish_back(upstream * mask)[0]
    gain_part = jnp.sum(inner * scaled, axis=0)
    shift_part = jnp.sum(inner, axis=0)
    direct = inner * gain
    first, second = lax.psum((jnp.sum(direct, axis=0), jnp.sum(direct * scaled, axis=0)), "bn")
    result = inverse * (direct - mask * (first / count + scaled * (second / count)))
    return (result.astype(jnp.bfloat16), gain_part, shift_part)


def reduce_grads(grads):
    wide = lax.axis_size("dp")
    group = lax.axis_size("bn")
    shapes = [g.shape for g in grads]
    flat = jnp.concatenate([g.reshape(wide * group, -1) for g in grads], axis=1)
    share = lax.psum_scatter(flat, ("dp", "bn"), scatter_dimension=0, tiled=True)
    joined = lax.all_gather(share, "bn", axis=0, tiled=True)
    rows = joined.shape[0]
    results = []
    offset = 0
    for shape in shapes:
        length = 1
        for extent in shape:
            length = length * extent
        columns = length // wide // rows
        piece = joined[:, offset : offset + columns]
        results.append(piece.reshape((shape[0] // wide,) + tuple(shape[1:])))
        offset = offset + columns
    return results


def local(
    images,
    image_count,
    image_size,
    cotangent,
    stem_weight,
    split_main,
    split_side,
    block_reduce,
    block_spatial,
    block_transit,
    merge_weight,
    affines,
):
    slots = images.shape[0]
    grid = cotangent.shape[1]
    width = merge_weight.shape[0]
    half = split_main.shape[1]
    places = jnp.arange(grid, dtype=jnp.int32)
    present = jnp.arange(slots, dtype=jnp.int32) < image_count[0]
    sizes = image_size[:, None, None]
    inside = (
        (places[None, :, None] < sizes) & (places[None, None, :] < sizes) & present[:, None, None]
    )
    mask = inside.astype(jnp.float32).reshape(-1, 1)
    local_count = jnp.sum(mask)
    gains = affines[:, 0]
    shifts = affines[:, 1]
    cuts = (0, width, width + half, width + 2 * half, 2 * width + 2 * half)
    stem_taps = stride_taps(images, grid)
    stem_pre = apply_taps(stem_taps, stem_weight)
    stem_act, stem_kept = normalize(
        stem_pre, mask, local_count, gains[cuts[0] : cuts[1]], shifts[cuts[0] : cuts[1]]
    )
    stem_low = stem_act.astype(jnp.bfloat16)
    main_path = matmul(stem_low, split_main)
    side_path = matmul(stem_low, split_side)
    main_low = main_path.astype(jnp.bfloat16)
    side_low = side_path.astype(jnp.bfloat16)
    reduce_pre = matmul(main_low, block_reduce)
    reduce_act, reduce_kept = normalize(
        reduce_pre, mask, local_count, gains[cuts[1] : cuts[2]], shifts[cuts[1] : cuts[2]]
    )
    reduce_low = reduce_act.astype(jnp.bfloat16)
    spatial_taps = unit_taps(reduce_low.reshape(slots, grid, grid, half), grid)
    spatial_pre = apply_taps(spatial_taps, block_spatial)
    spatial_act, spatial_kept = normalize(
        spatial_pre, mask, local_count, gains[cuts[2] : cuts[3]], shifts[cuts[2] : cuts[3]]
    )
    residual = main_path + spatial_act
    residual_low = residual.astype(jnp.bfloat16)
    transit_low = matmul(residual_low, block_transit).astype(jnp.bfloat16)
    merge_pre = matmul(transit_low, merge_weight[:half]) + matmul(side_low, merge_weight[half:])
    output, merge_kept = normalize(
        merge_pre, mask, local_count, gains[cuts[3] : cuts[4]], shifts[cuts[3] : cuts[4]]
    )
    activations = output.reshape(slots, grid, grid, width)
    upstream = cotangent.astype(jnp.float32).reshape(-1, width)
    merge_in, merge_gain, merge_shift = normalize_back(
        upstream, merge_kept, mask, gains[cuts[3] : cuts[4]]
    )
    grad_merge = jnp.concatenate(
        [outer_sum(transit_low, merge_in), outer_sum(side_low, merge_in)], axis=0
    )
    transit_back = against(merge_in, merge_weight[:half]).astype(jnp.bfloat16)
    side_back = against(merge_in, merge_weight[half:]).astype(jnp.bfloat16)
    grad_transit = outer_sum(residual_low, transit_back)
    residual_back = against(transit_back, block_transit)
    spatial_in, spatial_gain, spatial_shift = normalize_back(
        residual_back, spatial_kept, mask, gains[cuts[2] : cuts[3]]
    )
    grad_spatial = taps_grad(spatial_taps, spatial_in, block_spatial)
    reduce_back = unit_back(spatial_in, block_spatial, slots, grid)
    reduce_in, reduce_gain, reduce_shift = normalize_back(
        reduce_back, reduce_kept, mask, gains[cuts[1] : cuts[2]]
    )
    grad_reduce = outer_sum(main_low, reduce_in)
    main_back = (residual_back + against(reduce_in, block_reduce)).astype(jnp.bfloat16)
    grad_main = outer_sum(stem_low, main_back)
    grad_side = outer_sum(stem_low, side_back)
    stem_back = against(main_back, split_main) + against(side_back, split_side)
    stem_in, stem_gain, stem_shift = normalize_back(
        stem_back, stem_kept, mask, gains[cuts[0] : cuts[1]]
    )
    grad_stem = taps_grad(stem_taps, stem_in, stem_weight)
    image_grad = stride_back(stem_in, stem_weight, slots, grid)
    affine_grad = jnp.stack(
        [
            jnp.concatenate([stem_gain, reduce_gain, spatial_gain, merge_gain]),
            jnp.concatenate([stem_shift, reduce_shift, spatial_shift, merge_shift]),
        ],
        axis=1,
    )
    (
        grad_stem,
        grad_main,
        grad_side,
        grad_reduce,
        grad_spatial,
        grad_transit,
        grad_merge,
        affine_grad,
    ) = reduce_grads(
        [
            grad_stem,
            grad_main,
            grad_side,
            grad_reduce,
            grad_spatial,
            grad_transit,
            grad_merge,
            affine_grad,
        ]
    )
    return (
        activations,
        image_grad,
        grad_stem,
        grad_main,
        grad_side,
        grad_reduce,
        grad_spatial,
        grad_transit,
        grad_merge,
        affine_grad,
    )


def solution(mesh):
    return jax.shard_map(
        local,
        mesh=mesh,
        in_specs=(
            P(("dp", "bn"), None, None, None),
            P(("dp", "bn")),
            P(("dp", "bn")),
            P(("dp", "bn"), None, None, None),
            P(),
            P(),
            P(),
            P(),
            P(),
            P(),
            P(),
            P(),
        ),
        out_specs=(
            P(("dp", "bn"), None, None, None),
            P(("dp", "bn"), None, None, None),
            P("dp", None, None, None),
            P("dp", None),
            P("dp", None),
            P("dp", None),
            P("dp", None, None, None),
            P("dp", None),
            P("dp", None),
            P("dp", None),
        ),
        check_vma=False,
    )
```

profile of v0, /device:TPU:0, one launch (start us, length us, event | category | flops | bytes accessed | tf_op | source)
XLA Modules:
  0.0 1157.1 jit_solution(5852797519281649673)
XLA Ops:
  9.6 6.4 slice.224
  28.7 6.4 slice.218
  47.8 6.4 slice.212
  99.2 9.3 all-reduce.28
  189.3 6.9 all-reduce.24
  262.6 6.4 all-reduce.21
  280.1 38.6 %copy.40 = f32[512,9,1024]{2,1,0:T(8,128)} copy(f32[512,9,1024]{2,0,1:T(8,128)S(1)} %bitcast_dynamic-update-slice_fusion) | data formatting | bytes 37748736 | tf_op jit(solution)/shard_map/stack | solution.py:53
  318.7 25.6 %reshape_reshape.6 = f32[32,147456]{1,0:T(8,128)} reshape(f32[512,9,1024]{2,1,0:T(8,128)} %copy.40) | data formatting | bytes 37748736 | tf_op jit(solution)/shard_map/reshape;reshape | solution.py:109
  344.4 12.5 %constant_dynamic-update-slice_fusion.7 = f32[32,303296]{1,0:T(8,128)} fusion(f32[32,147456]{1,0:T(8,128)} %reshape_reshape.6), kind=kLoop, calls=%fused_computation.263 | loop fusion | bytes 37748736
  375.5 15.5 %copy.41 = f32[512,9,512]{2,1,0:T(8,128)} copy(f32[512,9,512]{2,0,1:T(8,128)} %fusion.16) | data formatting | bytes 18874368 | tf_op jit(solution)/shard_map/stack | solution.py:53
  391.0 9.6 reshape_reshape.7
  421.7 8.1 constant_dynamic-update-slice_fusion.3
  433.8 568.7 %all-reduce.31.cloned.1.call-done = f32[32,303296]{1,0:T(8,128)} async-done(((f32[32,303296]{1,0:T(8,128)}), f32[32,303296]{1,0:T(8,128)}) %all-reduce.31.cloned.1.call-update) | async-done | bytes 38821904
  1013.2 8.1 pad.105
  1023.3 8.0 pad.104
  1033.2 8.0 pad.102
  1043.2 8.1 pad.101
  1053.2 8.1 pad.75
  1063.2 8.2 pad.73
  1073.4 8.2 pad.74
  1083.6 8.1 pad.146
  1093.6 8.2 pad.145
  1106.8 11.8 %fusion.4 = f32[1,38,38,512]{3,2,1,0:T(8,128)} fusion(f32[1,38,38,512]{3,2,1,0:T(8,128)} %pad.105, f32[1,38,38,512]{3,2,1,0:T(8,128)} %pad.104, f32[1,38,38,512]{3,2,1,0:T(8,128)} %pad.102, f32[1,38,38,512]{3,2,1,0:T(8,128)} %pad.101, f32[1,40,40,512]{3,2,1,0:T(8,128)S(1)} %add_add_fusion, f32[1,38,39,512]{3,2,1,0:T(8,128)} %pad.146, f32[1,38,39,512]{3,2,1,0:T(8,128)} %pad.145), kind=kLoop, calls=%fused_computation.14 | loop fusion | flops 4435968 | bytes 23658496 | tf_op jit(solution)/shard_map/add | solution.py:63
  1118.6 6.5 copy.44
  (326 shorter events, 328.7 us)
Async XLA Ops:
  7.2 145.0 %copy-start = (bf16[1024,512]{1,0:T(8,128)(2,1)S(1)}, bf16[1024,512]{1,0:T(8,128)(2,1)}, u32[]{:S(2)}) copy-start(bf16[1024,512]{1,0:T(8,128)(2,1)} %param.20) | copy-start | bytes 3145732
  7.2 995.3 %all-reduce.31.cloned.1.call-start = ((), (), s32[]{:S(2)}) async-start(), calls=%async_computation.1 | async-start | bytes 77660160
  41.4 19.8 %copy-start.72 = (f32[3072,2]{0,1:T(2,128)S(1)}, f32[3072,2]{0,1:T(2,128)}, u32[]{:S(2)}) copy-start(f32[3072,2]{0,1:T(2,128)} %param.25) | copy-start | bytes 73732
  65.9 7.3 copy-start.38
  67.2 6.0 copy-start.40
  73.3 7.3 copy-start.42
  76.4 4.3 copy-start.61
  77.6 6.3 copy-start.44
  80.8 7.4 copy-start.46
  83.9 4.3 copy-start.60
  85.1 6.3 copy-start.48
  88.4 5.2 copy-start.50
  91.6 7.6 copy-start.52
  111.0 59.6 %copy-start.3 = (f32[361,512]{1,0:T(8,128)}, f32[361,512]{1,0:T(8,128)S(1)}, u32[]{:S(2)}) copy-start(f32[361,512]{1,0:T(8,128)S(1)} %fusion.137) | copy-start | bytes 2217988
  169.8 4.9 copy-start.65
  199.9 3.9 copy-start.10
  241.0 4.6 copy-start.22
  262.6 8.9 copy-start.51
  412.6 4.0 copy-start.7
  421.7 8.1 copy-start.20
  421.7 9.1 copy-start.2
  433.7 691.4 %all-gather.3.cloned.1.call-start = ((), (), s32[]{:S(2)}) async-start(), calls=%async_computation | async-start | bytes 6067200 | tf_op jit(solution)/shard_map/all_gather | solution.py:111
  433.8 574.6 %copy-start.16 = (f32[361,1024]{1,0:T(8,128)S(1)}, f32[361,1024]{1,0:T(8,128)}, u32[]{:S(2)}) copy-start(f32[361,1024]{1,0:T(8,128)} %get-tuple-element.114) | copy-start | bytes 4435972
  1143.5 6.6 copy-start.1
  (51 other events, 119.9 us)
Sparse Core Ops, SparseCore 0:
  433.9 568.5 all-reduce.30
  1008.2 37.0 all-gather.2
where the time goes:
time: 1170 us; the launch traced here: 1160 us
  waiting for transfers between devices  569 us (49%)
  local copies, waits for them, and re-layouts  344 us (29%)
  matrix products  123 us (11%)
  other arithmetic  53.4 us (5%)
  blocking collectives  52.1 us (4%)
  between operations  16.7 us (1%)
    unnamed x3, waiting for transfers between devices  569 us
    unnamed x161, local copies, waits for them, and re-layouts  73 us
    another operation x2, local copies, waits for them, and re-layouts, taps_grad(): stacked = jnp.stack([outer_sum(tap, upstream) for tap in taps], axis=1)  54.1 us
    slice x9, local copies, waits for them, and re-layouts, stride_taps(): padded[:, a:a + reach:2, b:b + reach:2, :].reshape(-1, field.shape[3])  51.6 us
    dot_general x24, matrix products, matmul(): return jnp.dot(left, right, preferred_element_type=jnp.float32)  51.6 us
    dot_general x24, matrix products, against(): lax.dot_general(left, right, (((1,), (1,)), ((), ())), preferred_element_...  40.2 us
    another operation x2, local copies, waits for them, and re-layouts, reduce_grads(): flat = jnp.concatenate([g.reshape(wide * group, -1) for g in grads], axis=1)  35.2 us
    slice x4, local copies, waits for them, and re-layouts, stride_back(): return result[:, 1:2 * grid + 1, 1:2 * grid + 1, :]  32.3 us
  transfers between devices with their start and end apart: 2, of which 1 were waited for; matrix products, arithmetic and copies ran while one was open for 10% of the time, Pallas kernels for 0%

commit v1 on v0

v1 whole, which is shorter than its diff:
```python
import functools

import jax
import jax.numpy as jnp
from jax import lax
from jax.experimental import pallas as pl
from jax.experimental.pallas import tpu as pltpu
from jax.sharding import PartitionSpec as P

EPS = 1e-05
F32 = jnp.float32
BF16 = jnp.bfloat16
MESH = pl.DeviceIdType.MESH
LEAD = 32
LANES = 128


def mish_parts(value):
    t = jnp.exp(-jnp.abs(value))
    positive = value >= 0
    t2 = t * t
    top = jnp.where(positive, 1.0 + 2.0 * t, t2 + 2.0 * t)
    inv = 1.0 / (top + jnp.where(positive, 2.0 * t2, 2.0))
    gate = top * inv
    slope = jnp.where(positive, t2, t) * (1.0 + t) * (4.0 * inv * inv)
    return value * gate, gate + value * slope


def dot(left, right):
    return jnp.dot(left, right, preferred_element_type=F32)


def dot_t(left, right):
    return lax.dot_general(left, right, (((1,), (1,)), ((), ())), preferred_element_type=F32)


def lane_tile(j, size=LANES):
    if isinstance(j, int):
        return pl.ds(j * size, size)
    return pl.ds(pl.multiple_of(j * size, size), size)


def share_order(n_dp):
    bits = [b for b in range(n_dp.bit_length() - 1)]
    if len(bits) < 2:
        return bits
    return [1, 0] + bits[:1:-1]


def share_place(share, n_dp):
    place = 0
    for bit in share_order(n_dp):
        place = 2 * place + (share >> bit) % 2
    return place


def flip(index, bit):
    low = lax.rem(index // (1 << bit), 2)
    return index + (1 - 2 * low) * (1 << bit), low


def chain_kernel(
    dims,
    count_ref, size_ref, images_ref, cot_ref, ws_hbm, wm_hbm, wsd_hbm, wr_hbm, w2_hbm, wt_hbm, wmg_hbm, aff_ref,
    act_ref, eo_hbm, ex_hbm, ao_hbm, ax_hbm, g0_ref, g2_ref,
    stem_low, joined, main_low, res_low, merge_in, tside, red_in, mside, sums_ref,
    ws, wms, wr, w2, wt, wmg, wsem,
    img_row, phases, taps, z0, d0, z1, d1, z2, d2, z3, i3, cot, main_path, apad, gpad, back, mask, stat,
    msg, heard, ssem, rsem, et, esem,
):
    grid, cin, width, half, n_dp, n_bn = dims
    pitch = grid + 1
    rows = z0.shape[0]
    share = cin // n_dp
    dp, bn = lax.axis_index("dp"), lax.axis_index("bn")
    others = [(dp, lax.rem(bn + k, n_bn)) for k in range(1, n_bn)]
    pair = (flip(dp, 1)[0], bn)
    act_bit = flip(dp, 1)[1]

    loads = [
        pltpu.make_async_copy(src, dst, wsem.at[k])
        for k, (src, dst) in enumerate(
            [(ws_hbm, ws), (wm_hbm, wms.at[:, pl.ds(0, half)]), (wsd_hbm, wms.at[:, pl.ds(half, half)]),
             (wr_hbm, wr), (w2_hbm, w2), (wt_hbm, wt), (wmg_hbm, wmg)]
        )
    ]
    for load in loads:
        load.start()

    barrier = pltpu.get_barrier_semaphore()
    for target in others + [pair]:
        pl.semaphore_signal(barrier, inc=1, device_id=target, device_id_type=MESH)

    places = lax.broadcasted_iota(jnp.int32, (rows, LANES), 0)
    row = (places * 3277) >> 16 if pitch == 20 else places // pitch
    col = places - row * pitch
    size = jnp.where(count_ref[0] > 0, size_ref[0], 0)
    mask[...] = jnp.where((row < size) & (col < size), 1.0, 0.0).astype(F32)

    for p in range(4):
        phases[p, 0:LEAD, :] = jnp.zeros((LEAD, cin), F32)
        tail = LEAD + pitch * grid
        phases[p, tail:, :] = jnp.zeros((phases.shape[1] - tail, cin), F32)
    for line in range(2 * grid):
        slot = line % 2
        value = images_ref[line].astype(F32)
        for k in range(cin // LANES):
            img_row[slot, k, 0 : 2 * grid, :] = value[:, k * LANES : (k + 1) * LANES]
        start = LEAD + pitch * (line // 2)
        for odd in range(2):
            p = 2 * (line % 2) + odd
            for k in range(cin // LANES):
                phases[p, start : start + grid, k * LANES : (k + 1) * LANES] = img_row[slot, k, pl.ds(odd, grid, stride=2), :]
            phases[p, start + grid : start + grid + 1, :] = jnp.zeros((1, cin), F32)

    for k in range(9):
        a, b = k // 3, k % 3
        p = 2 * (a != 1) + (b != 1)
        off = LEAD - pitch * (a == 0) - (b == 0)
        taps[:, k * cin : (k + 1) * cin] = phases[p, off : off + rows, :].astype(BF16)
    loads[0].wait()

    def put_sums(sync, j, first, second, tiles):
        msg[sync, pl.ds(j, 1), :] = first
        msg[sync, pl.ds(tiles + j, 1), :] = second

    def column_sums(sync, z, j, tiles):
        m = mask[...]
        zm = z * m
        put_sums(sync, j, jnp.sum(zm, axis=0, keepdims=True), jnp.sum(zm * z, axis=0, keepdims=True), tiles)

    def matmul_stats(sync, left, weight, out, cols):
        def body(n, _):
            z = dot(left[...], weight[:, lane_tile(n, 256)])
            out[:, lane_tile(n, 256)] = z
            for h in range(2):
                column_sums(sync, z[:, h * LANES : (h + 1) * LANES], 2 * n + h, cols // LANES)
            return 0
        lax.fori_loop(0, cols // 256, body, 0)

    def send(sync):
        heard[sync, bn] = msg[sync]
        copies = []
        for k, target in enumerate(others):
            copy = pltpu.make_async_remote_copy(
                src_ref=msg.at[sync], dst_ref=heard.at[sync, bn], send_sem=ssem.at[sync, k], recv_sem=rsem.at[sync, k],
                device_id=target, device_id_type=MESH,
            )
            copy.start()
            copies.append(copy)
        return copies

    def receive(sync, copies):
        for copy in copies:
            copy.wait()
        total = heard[sync, 0]
        for k in range(1, n_bn):
            total = total + heard[sync, k]
        return total

    def set_stat(slot, total, count, first_tile, tiles):
        mean = total[0:tiles] / count
        spread = total[tiles : 2 * tiles] / count - mean * mean
        stat[slot, 0, 0:tiles, :] = mean
        stat[slot, 1, 0:tiles, :] = lax.rsqrt(spread + EPS)
        for j in range(tiles):
            stat[slot, 2, j : j + 1, :] = aff_ref[2 * (first_tile + j) : 2 * (first_tile + j) + 1, :]
            stat[slot, 3, j : j + 1, :] = aff_ref[2 * (first_tile + j) + 1 : 2 * (first_tile + j) + 2, :]

    blocks = rows // LANES

    def per_tile(tiles, body):
        def step(j, _):
            body(j, lane_tile(j))
            return 0
        lax.fori_loop(0, tiles, step, 0)

    def normed(slot, z, j, cs, r):
        mean = stat[slot, 0, pl.ds(j, 1), :]
        inv = stat[slot, 1, pl.ds(j, 1), :]
        scaled = (z[r, cs] - mean) * inv
        return scaled, scaled * stat[slot, 2, pl.ds(j, 1), :] + stat[slot, 3, pl.ds(j, 1), :]

    def forward(slot, z, keep, tiles, put):
        def body(j, cs):
            for b in range(blocks):
                r = pl.ds(b * LANES, LANES)
                unused, before = normed(slot, z, j, cs, r)
                act, slope = mish_parts(before)
                keep[r, cs] = slope * mask[r, :]
                put(r, cs, act * mask[r, :])
        per_tile(tiles, body)

    def backward_sums(sync, slot, z, inner_ref, j, cs, upstream_of, tiles):
        first = jnp.zeros((1, LANES), F32)
        second = jnp.zeros((1, LANES), F32)
        for b in range(blocks):
            r = pl.ds(b * LANES, LANES)
            mean = stat[slot, 0, pl.ds(j, 1), :]
            inv = stat[slot, 1, pl.ds(j, 1), :]
            inner = inner_ref[r, cs] * upstream_of(r, cs)
            inner_ref[r, cs] = inner
            first = first + jnp.sum(inner, axis=0, keepdims=True)
            second = second + jnp.sum(inner * ((z[r, cs] - mean) * inv), axis=0, keepdims=True)
        put_sums(sync, j, first, second, tiles)

    def set_back(slot, total, count, first_tile, tiles):
        for j in range(tiles):
            sums_ref[2 * (first_tile + j) : 2 * (first_tile + j) + 1, :] = total[tiles + j : tiles + j + 1]
            sums_ref[2 * (first_tile + j) + 1 : 2 * (first_tile + j) + 2, :] = total[j : j + 1]
        stat[slot, 4, 0:tiles, :] = total[0:tiles] / count
        stat[slot, 5, 0:tiles, :] = total[tiles : 2 * tiles] / count

    def backward(slot, z, inner_ref, tiles, put):
        def body(j, cs):
            for b in range(blocks):
                r = pl.ds(b * LANES, LANES)
                mean = stat[slot, 0, pl.ds(j, 1), :]
                inv = stat[slot, 1, pl.ds(j, 1), :]
                scaled = (z[r, cs] - mean) * inv
                first = stat[slot, 4, pl.ds(j, 1), :]
                second = stat[slot, 5, pl.ds(j, 1), :]
                value = (inner_ref[r, cs] - mask[r, :] * (first + scaled * second)) * (inv * stat[slot, 2, pl.ds(j, 1), :])
                put(r, cs, value.astype(BF16))
        per_tile(tiles, body)

    wide_tiles, half_tiles = width // LANES, half // LANES
    t0, t1, t2, t3 = 0, wide_tiles, wide_tiles + half_tiles, wide_tiles + 2 * half_tiles

    matmul_stats(0, taps, ws, z0, width)
    msg[0, 2 * wide_tiles : 2 * wide_tiles + 8, :] = jnp.zeros((8, LANES), F32) + jnp.sum(mask[...], axis=0, keepdims=True)
    pl.semaphore_wait(barrier, n_bn)
    copies = send(0)

    def turn_phase(p, _):
        for k in range(cin // LANES):
            block = phases[p, LEAD : LEAD + rows, k * LANES : (k + 1) * LANES].T
            for s in range(k * LANES // share, (k + 1) * LANES // share):
                at = share_place(s, n_dp) * share
                inside = s * share - k * LANES
                et[p, at : at + share, :] = block[inside : inside + share, :]
        return 0
    lax.fori_loop(0, 4, turn_phase, 0)
    part = cin // 2
    mine = pl.ds(pl.multiple_of(act_bit * part, part), part)
    theirs = pl.ds(pl.multiple_of((1 - act_bit) * part, part), part)
    keep_e = pltpu.make_async_copy(et.at[0:4, mine, :], eo_hbm, esem.at[0])
    give_e = pltpu.make_async_remote_copy(
        src_ref=et.at[0:4, theirs, :], dst_ref=ex_hbm, send_sem=esem.at[1], recv_sem=esem.at[2],
        device_id=pair, device_id_type=MESH)
    keep_e.start()
    give_e.start()

    for r in range(grid):
        cot[r * pitch : r * pitch + grid, :] = cot_ref[r].astype(F32)
        cot[r * pitch + grid : (r + 1) * pitch, :] = jnp.zeros((1, width), F32)
    cot[grid * pitch :, :] = jnp.zeros((rows - grid * pitch, width), F32)
    apad[0:LEAD, :] = jnp.zeros((LEAD, half), F32)
    apad[LEAD + rows :, :] = jnp.zeros((LEAD, half), F32)
    gpad[0:LEAD, :] = jnp.zeros((LEAD, half), F32)
    gpad[LEAD + rows :, :] = jnp.zeros((LEAD, half), F32)

    total = receive(0, copies)
    count = total[2 * wide_tiles : 2 * wide_tiles + 1, 0:1]
    set_stat(0, total, count, t0, wide_tiles)

    def put_stem(r, cs, act):
        stem_low[r, cs] = act.astype(BF16)
    forward(0, z0, d0, wide_tiles, put_stem)
    loads[1].wait()
    loads[2].wait()
    for n in range(half // 256):
        y = dot(stem_low[...], wms[:, lane_tile(n, 256)])
        main_path[:, lane_tile(n, 256)] = y
        main_low[:, lane_tile(n, 256)] = y.astype(BF16)
    loads[3].wait()
    matmul_stats(1, main_low, wr, z1, half)
    copies = send(1)
    for n in range(half // 256):
        y = dot(stem_low[...], wms[:, lane_tile(half // 256 + n, 256)])
        joined[:, lane_tile(half // 256 + n, 256)] = y.astype(BF16)
    set_stat(1, receive(1, copies), count, t1, half_tiles)

    def put_reduce(r, cs, act):
        apad[pl.ds(LEAD + r.start, r.size), cs] = act.astype(BF16).astype(F32)
    forward(1, z1, d1, half_tiles, put_reduce)
    for k in range(9):
        off = LEAD + pitch * (k // 3 - 1) + k % 3 - 1
        taps[:, k * half : (k + 1) * half] = apad[off : off + rows, :].astype(BF16)
    loads[4].wait()
    matmul_stats(2, taps, w2, z2, half)
    copies = send(2)
    for k in range(half // LANES):
        block = apad[LEAD : LEAD + rows, k * LANES : (k + 1) * LANES].T
        for s in range(k * LANES // share, (k + 1) * LANES // share):
            at = share_place(s, n_dp) * share
            inside = s * share - k * LANES
            et[4, at : at + share, :] = block[inside : inside + share, :]
    keep_a = pltpu.make_async_copy(et.at[4, mine, :], ao_hbm, esem.at[3])
    give_a = pltpu.make_async_remote_copy(
        src_ref=et.at[4, theirs, :], dst_ref=ax_hbm, send_sem=esem.at[4], recv_sem=esem.at[5],
        device_id=pair, device_id_type=MESH)
    keep_a.start()
    give_a.start()
    set_stat(2, receive(2, copies), count, t2, half_tiles)

    def put_spatial(r, cs, act):
        res_low[r, cs] = (main_path[r, cs] + act).astype(BF16)
    forward(2, z2, d2, half_tiles, put_spatial)
    loads[5].wait()
    for n in range(half // 256):
        joined[:, lane_tile(n, 256)] = dot(res_low[...], wt[:, lane_tile(n, 256)]).astype(BF16)
    loads[6].wait()
    matmul_stats(3, joined, wmg, z3, width)
    set_stat(3, receive(3, send(3)), count, t3, wide_tiles)

    def merge_tile(j, cs):
        for b in range(blocks):
            r = pl.ds(b * LANES, LANES)
            unused, before = normed(3, z3, j, cs, r)
            act, slope = mish_parts(before)
            back[r, pl.ds(0, LANES)] = act * mask[r, :]
            i3[r, cs] = slope * mask[r, :]
        for line in range(grid):
            act_ref[pl.ds(line * grid * wide_tiles + j, grid, stride=wide_tiles), :] = back[line * pitch : line * pitch + grid, 0:LANES]
        backward_sums(4, 3, z3, i3, j, cs, lambda r, c: cot[r, c], wide_tiles)
    per_tile(wide_tiles, merge_tile)
    set_back(3, receive(4, send(4)), count, t3, wide_tiles)

    def put_merge(r, cs, value):
        merge_in[r, cs] = value
    backward(3, z3, i3, wide_tiles, put_merge)
    for n in range(width // 256):
        tside[:, lane_tile(n, 256)] = dot_t(merge_in[...], wmg[lane_tile(n, 256), :]).astype(BF16)
    for n in range(half // 256):
        back[:, lane_tile(n, 256)] = dot_t(tside[:, 0:half], wt[lane_tile(n, 256), :])

    def spatial_tile(j, cs):
        backward_sums(5, 2, z2, d2, j, cs, lambda r, c: back[r, c], half_tiles)
    per_tile(half_tiles, spatial_tile)
    set_back(2, receive(5, send(5)), count, t2, half_tiles)

    def put_spatial_in(r, cs, value):
        gpad[pl.ds(LEAD + r.start, r.size), cs] = value.astype(F32)
        g2_ref[r, cs] = value.astype(F32)
    backward(2, z2, d2, half_tiles, put_spatial_in)
    for k in range(9):
        off = LEAD - pitch * (k // 3 - 1) - (k % 3 - 1)
        taps[:, k * half : (k + 1) * half] = gpad[off : off + rows, :].astype(BF16)

    def reduce_columns(n, _):
        value = jnp.zeros((rows, 256), F32)
        for k in range(9):
            value = value + dot_t(taps[:, k * half : (k + 1) * half], w2[pl.ds(pl.multiple_of(k * half + n * 256, 256), 256), :])
        main_path[:, lane_tile(n, 256)] = value
        return 0
    lax.fori_loop(0, half // 256, reduce_columns, 0)

    def reduce_tile(j, cs):
        backward_sums(6, 1, z1, d1, j, cs, lambda r, c: main_path[r, c], half_tiles)
    per_tile(half_tiles, reduce_tile)
    copies = send(6)
    mside[:, half : 2 * half] = tside[:, half : 2 * half]
    set_back(1, receive(6, copies), count, t1, half_tiles)

    def put_reduce_in(r, cs, value):
        red_in[r, cs] = value
    backward(1, z1, d1, half_tiles, put_reduce_in)
    for n in range(half // 256):
        mside[:, lane_tile(n, 256)] = (back[:, lane_tile(n, 256)] + dot_t(red_in[...], wr[lane_tile(n, 256), :])).astype(BF16)

    def stem_columns(n, _):
        z3[:, lane_tile(n, 256)] = dot_t(mside[...], wms[lane_tile(n, 256), :])
        return 0
    lax.fori_loop(0, width // 256, stem_columns, 0)

    def stem_tile(j, cs):
        backward_sums(7, 0, z0, d0, j, cs, lambda r, c: z3[r, c], wide_tiles)
    per_tile(wide_tiles, stem_tile)
    set_back(0, receive(7, send(7)), count, t0, wide_tiles)

    def put_stem_in(r, cs, value):
        g0_ref[r, cs] = value.astype(F32)
    backward(0, z0, d0, wide_tiles, put_stem_in)
    keep_e.wait()
    keep_a.wait()
    give_e.wait()
    give_a.wait()


def chain(dims, count, size, images, cot, ws, wm, wsd, wr, w2, wt, wmg, aff):
    grid, cin, width, half, n_dp, n_bn = dims
    rows = -(-grid * (grid + 1) // LANES) * LANES
    sd = jax.ShapeDtypeStruct
    part = cin // 2
    tiles = width // LANES
    out = (
        sd((grid * grid * tiles, LANES), F32),
        sd((4, part, rows), F32), sd((4, part, rows), F32), sd((half // 2, rows), F32), sd((half // 2, rows), F32),
        sd((rows, width), F32), sd((rows, half), F32),
        sd((rows, width), BF16), sd((rows, 2 * half), BF16), sd((rows, half), BF16), sd((rows, half), BF16),
        sd((rows, width), BF16), sd((rows, 2 * half), BF16), sd((rows, half), BF16), sd((rows, 2 * half), BF16),
        sd(aff.shape, F32),
    )
    vm, any_ = pl.BlockSpec(memory_space=pltpu.VMEM), pl.BlockSpec(memory_space=pl.ANY)
    sm = pl.BlockSpec(memory_space=pltpu.SMEM)
    scratch = [
        pltpu.VMEM((9 * cin, width), BF16), pltpu.VMEM((width, 2 * half), BF16), pltpu.VMEM((half, half), BF16),
        pltpu.VMEM((9 * half, half), BF16), pltpu.VMEM((half, half), BF16), pltpu.VMEM((width, width), BF16),
        pltpu.SemaphoreType.DMA((7,)),
        pltpu.VMEM((2, cin // LANES, -(-2 * grid // 8) * 8, LANES), F32),
        pltpu.VMEM((4, LEAD + rows, cin), F32),
        pltpu.VMEM((rows, 9 * cin), BF16),
        pltpu.VMEM((rows, width), F32), pltpu.VMEM((rows, width), F32),
        pltpu.VMEM((rows, half), F32), pltpu.VMEM((rows, half), F32),
        pltpu.VMEM((rows, half), F32), pltpu.VMEM((rows, half), F32),
        pltpu.VMEM((rows, width), F32), pltpu.VMEM((rows, width), F32),
        pltpu.VMEM((rows, width), F32),
        pltpu.VMEM((rows, half), F32),
        pltpu.VMEM((LEAD + rows + LEAD, half), F32), pltpu.VMEM((LEAD + rows + LEAD, half), F32),
        pltpu.VMEM((rows, half), F32),
        pltpu.VMEM((rows, LANES), F32),
        pltpu.VMEM((4, 6, 8, LANES), F32),
        pltpu.VMEM((8, 3 * tiles, LANES), F32), pltpu.VMEM((8, n_bn, 3 * tiles, LANES), F32),
        pltpu.SemaphoreType.DMA((8, n_bn - 1)), pltpu.SemaphoreType.DMA((8, n_bn - 1)),
        pltpu.VMEM((5, cin, rows), F32), pltpu.SemaphoreType.DMA((6,)),
    ]
    return pl.pallas_call(
        functools.partial(chain_kernel, dims),
        out_shape=out,
        in_specs=[sm, sm, vm, vm] + [any_] * 7 + [vm],
        out_specs=(vm,) + (any_,) * 4 + (vm,) * 11,
        scratch_shapes=scratch,
        compiler_params=pltpu.CompilerParams(collective_id=0, has_side_effects=True, vmem_limit_bytes=63 * 2**20),
        name="chain",
    )(count, size, images, cot, ws, wm, wsd, wr, w2, wt, wmg, aff)


N_SPATIAL, N_STEM, N_DENSE = 5, 9, 5


def grads_kernel(
    dims,
    eo_hbm, ex_hbm, ao_hbm, ax_hbm, g0_hbm, g2_hbm,
    stem_hbm, joined_hbm, main_hbm, res_hbm, merge_hbm, tside_hbm, red_hbm, mside_hbm, sums_ref, ws_hbm,
    igrad_ref, out_hbm, total_ref, ec_hbm, ac_hbm,
    g0r, g2r, at_land, at_cat, et_land, et_cat, units, cuts_a, last_a, cuts_b, pair_b, cross_b, own_g, sums_in,
    load_sem, give_sem, take_sem, a_send, a_recv, b_send, b_recv, out_sem, s_send, s_recv,
):
    grid, cin, width, half, n_dp, n_bn = dims
    pitch = grid + 1
    rows = at_cat.shape[1] // 4
    share = cin // n_dp
    part = cin // 2
    dp, bn = lax.axis_index("dp"), lax.axis_index("bn")
    order = share_order(n_dp)
    order_a = order[1:]
    sib, core = flip(bn, 0)
    over, cross = flip(bn, 1)
    act_dp, act_bit = flip(dp, 1)
    partners = [(dp, sib), (dp, over), (act_dp, bn), (act_dp, sib)] + [(flip(dp, b)[0], bn) for b in order_a]
    bit_of = {b: flip(dp, b) for b in order}

    barrier = pltpu.get_barrier_semaphore()
    for target in partners:
        pl.semaphore_signal(barrier, inc=1, device_id=target, device_id_type=MESH)
    pl.semaphore_wait(barrier, len(partners))

    def remote(src, dst, send, recv, target):
        return pltpu.make_async_remote_copy(
            src_ref=src, dst_ref=dst, send_sem=send, recv_sem=recv, device_id=target, device_id_type=MESH)

    half2, half0 = half // 2, width // 2

    def cols(which, size):
        return pl.ds(pl.multiple_of(which * size, size), size)

    gives = []
    fields = ((g2_hbm, g2r, half2), (g0_hbm, g0r, half0))
    for f, (src, dst, size) in enumerate(fields):
        lead = LEAD if f == 0 else 0
        for k, (target, which) in enumerate((((dp, sib), 1 - core), ((act_dp, bn), core), ((act_dp, sib), 1 - core))):
            gives.append(remote(
                src.at[:, cols(which, size)], dst.at[k + 1, pl.ds(lead, rows)],
                give_sem.at[3 * f + k], take_sem.at[3 * f + k], target))
    forwards = [
        remote(ao_hbm, ac_hbm.at[0], give_sem.at[6], take_sem.at[6], (dp, sib)),
        remote(ax_hbm, ac_hbm.at[1], give_sem.at[7], take_sem.at[7], (dp, sib)),
        remote(eo_hbm, ec_hbm.at[0], give_sem.at[8], take_sem.at[8], (dp, sib)),
        remote(ex_hbm, ec_hbm.at[1], give_sem.at[9], take_sem.at[9], (dp, sib)),
    ]
    locals_ = [
        pltpu.make_async_copy(g2_hbm.at[:, cols(core, half2)], g2r.at[0, pl.ds(LEAD, rows)], load_sem.at[0]),
        pltpu.make_async_copy(g0_hbm.at[:, cols(core, half0)], g0r.at[0, pl.ds(0, rows)], load_sem.at[1]),
        pltpu.make_async_copy(g0_hbm, own_g.at[pl.ds(0, rows)], load_sem.at[2]),
        pltpu.make_async_copy(ao_hbm, at_land.at[0], load_sem.at[3]),
        pltpu.make_async_copy(ax_hbm, at_land.at[1], load_sem.at[4]),
    ]
    for k in (0, 1, 2):
        gives[k].start()
    forwards[0].start()
    forwards[1].start()
    for k in (3, 4, 5):
        gives[k].start()
    forwards[2].start()
    forwards[3].start()
    for load in locals_:
        load.start()

    def sums_step(k):
        return remote(total_ref if k else sums_ref, sums_in.at[k], s_send.at[k], s_recv.at[k], (bit_of[order[k]][0], bn))

    def sums_next(k):
        sums_step(k).wait()
        total_ref[...] = (total_ref[...] if k else sums_ref[...]) + sums_in[k]
        if k + 1 < len(order):
            sums_step(k + 1).start()
    sums_step(0).start()

    for k in range(4):
        g2r[k, 0:LEAD, :] = jnp.zeros((LEAD, half2), F32)
        g2r[k, LEAD + rows :, :] = jnp.zeros((LEAD, half2), F32)
        g0r[k, rows:, :] = jnp.zeros((LEAD, half0), F32)
    own_g[rows:, :] = jnp.zeros((LEAD, width), F32)

    n_b = len(order)

    def b_core(u, full):
        return remote(full.at[u % 2, :, cols(1 - core, half0)], pair_b.at[u], b_send.at[0, u], b_recv.at[0, u], (dp, sib))

    def b_cross(u):
        return remote(pair_b.at[u, :, cols(1 - cross, 256)], cross_b.at[u], b_send.at[1, u], b_recv.at[1, u], (dp, over))

    def b_step(u, i):
        src = cross_b if i == 0 else cuts_b[i - 1]
        size = cuts_b[i].shape[1]
        partner, bit = bit_of[order[i]]
        at = pl.ds(pl.multiple_of((1 - bit) * size, size), size)
        return remote(src.at[u, at], cuts_b[i].at[u], b_send.at[2 + i, u], b_recv.at[2 + i, u], (partner, bn))

    def add_rows(dst, src, size):
        n = min(size, 64)

        def body(k, _):
            r = pl.ds(pl.multiple_of(k * n, n), n)
            dst(r)
            return 0
        lax.fori_loop(0, size // n, body, 0)

    def b_after_core(u, full):
        b_core(u, full).wait()

        def add(r):
            pair_b[u, r, :] = pair_b[u, r, :] + full[u % 2, r, cols(core, half0)]
        add_rows(add, None, cin)
        b_cross(u).start()

    def b_after(u, i):
        if i == 0:
            b_cross(u).wait()

            def add(r):
                cross_b[u, r, :] = cross_b[u, r, :] + pair_b[u, r, cols(cross, 256)]
            add_rows(add, None, cin)
        else:
            b_step(u, i - 1).wait()
            src = cross_b if i == 1 else cuts_b[i - 2]
            dst = cuts_b[i - 1]
            size = dst.shape[1]
            bit = bit_of[order[i - 1]][1]

            def add(r):
                at = pl.ds(pl.multiple_of(bit * size + r.start, 8), r.size)
                dst[u, r, :] = dst[u, r, :] + src[u, at, :]
            add_rows(add, None, size)
        if i < n_b:
            b_step(u, i).start()

    def place(at):
        return cols(2 * core + at, 256)

    def gather_cross(u, src):
        mine = out_hbm.at[u, :, place(cross)]
        return (
            pltpu.make_async_copy(src, mine, out_sem.at[0, u]),
            remote(src, mine, out_sem.at[1, u], out_sem.at[2, u], (dp, over)),
        )

    def gather_core(u):
        both = out_hbm.at[u, :, cols(core, half0)]
        return remote(both, both, out_sem.at[3, u], out_sem.at[4, u], (dp, sib))

    def dense_phase(full, turned, r_merge, r_tside, r_red, r_mside, land):
        ins = ((joined_hbm, land, 2), (res_hbm, land, 1), (main_hbm, land, 1), (stem_hbm, land, 2))
        rights = [pltpu.make_async_copy(s, d, load_sem.at[5 + k]) for k, (s, d) in enumerate(
            ((merge_hbm, r_merge), (tside_hbm, r_tside), (red_hbm, r_red), (mside_hbm, r_mside)))]
        for load in rights:
            load.start()

        def turn(src, first, parts):
            size = parts * half
            load = pltpu.make_async_copy(src, land.at[:, pl.ds(0, size)], load_sem.at[9])
            load.start()
            load.wait()
            for k in range(size // LANES):
                block = land[:, k * LANES : (k + 1) * LANES].astype(F32).T
                for piece in range(LANES // share):
                    row = k * LANES + piece * share
                    s, h = (row // share) // parts, (row // share) % parts
                    at = share_place(s, n_dp) * share
                    turned[first + h, at : at + share, :] = block[piece * share : (piece + 1) * share].astype(BF16)

        def fill(u, left, right_ref, lo, hi):
            for n in range((hi - lo) // 256):
                full[u % 2, :, pl.ds(lo + n * 256, 256)] = dot(turned[left], right_ref[:, pl.ds(lo_of(right_ref, lo) + n * 256, 256)])

        def lo_of(ref, lo):
            return lo if ref.shape[1] >= width else 0

        turn(joined_hbm, 0, 2)
        rights[0].wait()
        fill(0, 0, r_merge, 0, width)
        b_core(0, full).start()
        fill(1, 1, r_merge, 0, width)
        b_core(1, full).start()
        turn(res_hbm, 2, 1)
        turn(main_hbm, 3, 1)
        b_after_core(0, full)
        rights[1].wait()
        rights[2].wait()
        fill(2, 2, r_tside, 0, half)
        fill(2, 3, r_red, half, 2 * half)
        b_core(2, full).start()
        b_after_core(1, full)
        turn(stem_hbm, 4, 2)
        rights[3].wait()
        fill(3, 4, r_mside, 0, width)
        b_core(3, full).start()
        b_after_core(2, full)
        fill(4, 5, r_mside, 0, width)
        b_core(4, full).start()
        b_after_core(3, full)
        b_after_core(4, full)

    pl.run_scoped(
        dense_phase, pltpu.VMEM((2, cin, width), F32), pltpu.VMEM((6, cin, rows), BF16),
        pltpu.VMEM((rows, width), BF16), pltpu.VMEM((rows, 2 * half), BF16), pltpu.VMEM((rows, half), BF16),
        pltpu.VMEM((rows, 2 * half), BF16), pltpu.VMEM((rows, width), BF16))

    n_a = len(order_a)
    n_units = N_SPATIAL + N_STEM

    def a_step(u, i):
        src = units.at[lax.rem(u, 3)] if i == 0 else cuts_a[i - 1].at[u]
        size = cuts_a[i].shape[1]
        partner, bit = bit_of[order_a[i]]
        at = pl.ds(pl.multiple_of((1 - bit) * size, size), size)
        return remote(src.at[at], cuts_a[i].at[u], a_send.at[i, u], a_recv.at[i, u], (partner, bn))

    def a_cross(u):
        return remote(cuts_a[-1].at[u, :, cols(1 - cross, 256)], last_a.at[u], a_send.at[n_a, u], a_recv.at[n_a, u], (dp, over))

    def a_after(u, i):
        if i < n_a:
            a_step(u, i).wait()
            dst = cuts_a[i]
            size = dst.shape[1]
            bit = bit_of[order_a[i]][1]

            def add(r):
                at = pl.ds(pl.multiple_of(bit * size + r.start, 8), r.size)
                own = units[lax.rem(u, 3), at, :] if i == 0 else cuts_a[i - 1][u, at, :]
                dst[u, r, :] = dst[u, r, :] + own
            add_rows(add, None, size)
            if i + 1 < n_a:
                a_step(u, i + 1).start()
            else:
                a_cross(u).start()
        elif i == n_a:
            a_cross(u).wait()
            last_a[u] = last_a[u] + cuts_a[-1][u, :, cols(cross, 256)]
            for copy in gather_cross(u, last_a.at[u]):
                copy.start()
        elif i == n_a + 1:
            for copy in gather_cross(u, last_a.at[u]):
                copy.wait()
            gather_core(u).start()
        else:
            gather_core(u).wait()

    n_stage = n_a + 3

    def advance(t, known):
        for i in range(n_stage):
            if isinstance(t, int):
                if 0 <= t - 1 - i < n_units:
                    a_after(t - 1 - i, i)
            elif i + 1 <= known:
                a_after(t - 1 - i, i)
            else:
                @pl.when(t - 1 - i >= 0)
                def _(i=i):
                    a_after(t - 1 - i, i)

    for load in locals_:
        load.wait()
    for k in (0, 1):
        forwards[k].wait()
        load = pltpu.make_async_copy(ac_hbm.at[k], at_land.at[2 + k], load_sem.at[10])
        load.start()
        load.wait()
    for k in (0, 1, 2):
        gives[k].wait()
    for slot, land in enumerate((0, 2, 1, 3)):
        at_cat[:, slot * rows : (slot + 1) * rows] = at_land[land].astype(BF16)
    sums_next(0)
    for u in range(N_SPATIAL):
        for h in range(2):
            k = 2 * u + h
            if k < 9:
                off = LEAD - pitch * (k // 3 - 1) - (k % 3 - 1)
                right = jnp.concatenate([g2r[s, off : off + rows, :].astype(BF16) for s in range(4)], axis=0)
                value = dot(at_cat[...], right)
            else:
                value = jnp.zeros((part, half2), F32)
            for x in range(2):
                units[u % 3, :, 256 * x + LANES * h : 256 * x + LANES * (h + 1)] = value[:, LANES * x : LANES * (x + 1)]
        a_step(u, 0).start()
        advance(u, 0)
    for u in range(N_DENSE):
        b_after(u, 0)
    sums_next(1)

    def stem_phase(shifted, own_shift, image, weight, wsem):
        def load_w(k):
            return pltpu.make_async_copy(
                ws_hbm.at[pl.ds(pl.multiple_of(k * cin, cin), cin)], weight.at[lax.rem(k, 2)], wsem.at[lax.rem(k, 2)])
        load_w(0).start()
        for k in (2, 3):
            forwards[k].wait()
        for p in range(4):
            pieces = [pltpu.make_async_copy(src, et_land.at[s], load_sem.at[11 + s]) for s, src in enumerate(
                (eo_hbm.at[p], ec_hbm.at[0, p], ex_hbm.at[p], ec_hbm.at[1, p]))]
            for piece in pieces:
                piece.start()
            for s, piece in enumerate(pieces):
                piece.wait()
                et_cat[p, :, s * rows : (s + 1) * rows] = et_land[s].astype(BF16)
            image[p] = jnp.zeros(image.shape[1:], F32)
        for sh, off in enumerate((0, 1, pitch, pitch + 1)):
            own_shift[sh] = own_g[off : off + rows, :].astype(BF16)
        for k in (3, 4, 5):
            gives[k].wait()
        for sh, off in enumerate((0, 1, pitch, pitch + 1)):
            for s in range(4):
                shifted[sh, s * rows : (s + 1) * rows, :] = g0r[s, off : off + rows, :].astype(BF16)

        def slot(k, _):
            a, b = k // 3, lax.rem(k, 3)
            p = 2 * jnp.where(a == 1, 0, 1) + jnp.where(b == 1, 0, 1)
            sh = 2 * jnp.where(a == 0, 1, 0) + jnp.where(b == 0, 1, 0)
            u = N_SPATIAL + k
            for n in range(half0 // 256):
                units[lax.rem(u, 3), :, n * 256 : (n + 1) * 256] = dot(et_cat[p], shifted[sh, :, n * 256 : (n + 1) * 256])
            a_step(u, 0).start()

            @pl.when(k < 8)
            def _():
                load_w(k + 1).start()
            load_w(k).wait()
            for n in range(cin // 256):
                c = slice(n * 256, (n + 1) * 256)
                image[p, :, c] = image[p, :, c] + dot_t(own_shift[sh], weight[lax.rem(k, 2), c, :])
            advance(u, N_SPATIAL)
            return 0

        lax.fori_loop(0, 3, slot, 0)
        for u in range(N_DENSE):
            b_after(u, 1)
        lax.fori_loop(3, 6, slot, 0)
        for u in range(N_DENSE):
            b_after(u, 2)
        lax.fori_loop(6, 9, slot, 0)

        def spread(p, _):
            pr, pc = p // 2, lax.rem(p, 2)
            for r in range(grid):
                for k in range(cin // LANES):
                    start = ((2 * r + pr) * 2 * grid + pc) * (cin // LANES) + k
                    igrad_ref[pl.ds(start, grid, stride=2 * cin // LANES), :] = image[p, r * pitch : r * pitch + grid, k * LANES : (k + 1) * LANES]
            return 0
        lax.fori_loop(0, 4, spread, 0)

    pl.run_scoped(
        stem_phase, pltpu.VMEM((4, 4 * rows, half0), BF16), pltpu.VMEM((4, rows, width), BF16),
        pltpu.VMEM((4, rows, cin), F32), pltpu.VMEM((2, cin, width), BF16), pltpu.SemaphoreType.DMA((2,)))

    for i in range(3, n_b + 1):
        for u in range(N_DENSE):
            b_after(u, i)
    for k in range(2, len(order)):
        sums_next(k)
    final = cuts_b[-1]
    for u in range(N_DENSE):
        for copy in gather_cross(n_units + u, final.at[u]):
            copy.start()
    for t in range(n_units, n_units + n_stage):
        advance(t, 0)
    for u in range(N_DENSE):
        for copy in gather_cross(n_units + u, final.at[u]):
            copy.wait()
        gather_core(n_units + u).start()
    for u in range(N_DENSE):
        gather_core(n_units + u).wait()


def grads(dims, eo, ex, ao, ax, g0, g2, stem_low, joined, main_low, res_low, merge_in, tside, red_in, mside, sums, ws):
    grid, cin, width, half, n_dp, n_bn = dims
    rows = g0.shape[0]
    share = cin // n_dp
    part = cin // 2
    n_units = N_SPATIAL + N_STEM
    sd = jax.ShapeDtypeStruct
    vm, any_ = pl.BlockSpec(memory_space=pltpu.VMEM), pl.BlockSpec(memory_space=pl.ANY)
    n_bits = len(share_order(n_dp))
    half0, half2 = width // 2, half // 2
    dma = pltpu.SemaphoreType.DMA
    scratch = [
        pltpu.VMEM((4, rows + LEAD, half0), F32), pltpu.VMEM((4, LEAD + rows + LEAD, half2), F32),
        pltpu.VMEM((4, part, rows), F32), pltpu.VMEM((part, 4 * rows), BF16),
        pltpu.VMEM((4, part, rows), F32), pltpu.VMEM((4, part, 4 * rows), BF16),
        pltpu.VMEM((3, part, half0), F32),
        [pltpu.VMEM((n_units, part >> (i + 1), half0), F32) for i in range(n_bits - 1)],
        pltpu.VMEM((n_units, share, 256), F32),
        [pltpu.VMEM((N_DENSE, cin >> (i + 1), 256), F32) for i in range(n_bits)],
        pltpu.VMEM((N_DENSE, cin, half0), F32), pltpu.VMEM((N_DENSE, cin, 256), F32),
        pltpu.VMEM((rows + LEAD, width), F32),
        pltpu.VMEM((n_bits,) + sums.shape, F32),
        dma((16,)), dma((10,)), dma((10,)),
        dma((n_bits, n_units)), dma((n_bits, n_units)), dma((n_bits + 2, N_DENSE)), dma((n_bits + 2, N_DENSE)),
        dma((5, n_units + N_DENSE)), dma((n_bits,)), dma((n_bits,)),
    ]
    out = (
        sd((4 * grid * grid * (cin // LANES), LANES), F32),
        sd((n_units + N_DENSE, share, width), F32),
        sd(sums.shape, F32),
        sd((2, 4, part, rows), F32), sd((2, part, rows), F32),
    )
    return pl.pallas_call(
        functools.partial(grads_kernel, dims),
        out_shape=out,
        in_specs=[any_] * 14 + [vm, any_],
        out_specs=(vm, any_, vm, any_, any_),
        scratch_shapes=scratch,
        compiler_params=pltpu.CompilerParams(collective_id=1, has_side_effects=True, vmem_limit_bytes=63 * 2**20),
        name="grads",
    )(eo, ex, ao, ax, g0, g2, stem_low, joined, main_low, res_low, merge_in, tside, red_in, mside, sums, ws)


def local(
    images, image_count, image_size, cotangent, stem_weight, split_main, split_side,
    block_reduce, block_spatial, block_transit, merge_weight, affines,
):
    n_dp, n_bn = lax.axis_size("dp"), lax.axis_size("bn")
    grid, cin = cotangent.shape[1], images.shape[3]
    width, half = merge_weight.shape[0], split_main.shape[1]
    share = cin // n_dp
    dims = (grid, cin, width, half, n_dp, n_bn)
    ws = stem_weight.transpose(1, 2, 0, 3).reshape(9 * cin, width)
    w2 = block_spatial.transpose(1, 2, 0, 3).reshape(9 * half, half)
    aff = affines.reshape(-1, LANES, 2).transpose(0, 2, 1).reshape(-1, LANES)
    act, *kept = chain(
        dims, image_count, image_size, images[0], cotangent[0], ws, split_main, split_side,
        block_reduce, w2, block_transit, merge_weight, aff)
    igrad, out, sums, unused, unused2 = grads(dims, *kept, ws)
    activations = act.reshape(1, grid, grid, width)
    image_grad = igrad.reshape(1, 2 * grid, 2 * grid, cin)
    grad_stem = out[N_SPATIAL : N_SPATIAL + N_STEM].reshape(3, 3, share, width).transpose(2, 0, 1, 3)
    spatial = out[:N_SPATIAL].reshape(N_SPATIAL, share, 4, 2, LANES).transpose(0, 3, 1, 2, 4)
    spatial = spatial.reshape(2 * N_SPATIAL, share, half)[:9]
    grad_spatial = spatial.reshape(3, 3, share, half).transpose(2, 0, 1, 3)
    dense = out[N_SPATIAL + N_STEM :]
    grad_merge = dense[0:2].transpose(0, 1, 2).reshape(2 * share, width)
    grad_transit, grad_reduce = dense[2, :, :half], dense[2, :, half:]
    split = dense[3:5].reshape(2 * share, width)
    grad_main, grad_side = split[:, :half], split[:, half:]
    mine = affines.shape[0] // n_dp
    whole = sums.reshape(-1, 2, LANES).transpose(0, 2, 1).reshape(-1, 2)
    affine_grad = lax.dynamic_slice_in_dim(whole, lax.axis_index("dp") * mine, mine, axis=0)
    return (activations, image_grad, grad_stem, grad_main, grad_side, grad_reduce, grad_spatial, grad_transit, grad_merge, affine_grad)


def solution(mesh):
    rows = P(("dp", "bn"), None, None, None)
    return jax.shard_map(
        local,
        mesh=mesh,
        in_specs=(rows, P(("dp", "bn")), P(("dp", "bn")), rows) + (P(),) * 8,
        out_specs=(
            rows, rows, P("dp", None, None, None), P("dp", None), P("dp", None), P("dp", None),
            P("dp", None, None, None), P("dp", None), P("dp", None), P("dp", None),
        ),
        check_vma=False,
    )
```

time: 1170 us -> 292 us (0.25); the launches traced: 1160 us -> 291 us
  waiting for transfers between devices: 569 us -> 0 us
  local copies, waits for them, and re-layouts: 344 us -> 19 us
  Pallas kernels: 0 us -> 270 us
  matrix products: 123 us -> 0 us
  other arithmetic: 53.4 us -> 0 us
  blocking collectives: 52.1 us -> 0 us
  between operations: 16.7 us -> 1.99 us
    unnamed x3 -> x0, waiting for transfers between devices: 569 us -> none
    pallas_call x0 -> x2, Pallas kernels: none -> 270 us  [the longest x1 209 us: grads(): pl.pallas_call(functools.partial(grads_kernel, dims), out_shape=out, in_s...]
    dot_general x72 -> x0, matrix products: 123 us -> none  [the longest x24 51.6 us: matmul(): return jnp.dot(left, right, preferred_element_type=jnp.float32)]
    another operation x7 -> x0, local copies, waits for them, and re-layouts: 91.4 us -> none  [the longest x2 54.1 us: taps_grad(): stacked = jnp.stack([outer_sum(tap, upstream) for tap in taps], axis=1)]
    slice x22 -> x5, local copies, waits for them, and re-layouts: 91.7 us -> 8.83 us  [the longest x1 3.36 us: local(): out[N_SPATIAL:N_SPATIAL + N_STEM].reshape(3, 3, share, width)]
    unnamed x161 -> x4, local copies, waits for them, and re-layouts: 73 us -> 5.1 us
    reshape x35 -> x3, local copies, waits for them, and re-layouts: 59.7 us -> 1.98 us  [the longest x2 1.45 us: local(): out[:N_SPATIAL].reshape(N_SPATIAL, share, 4, 2, LANES)]
    psum x8 -> x0, blocking collectives: 52.1 us -> none  [the longest x4 26.7 us: normalize(): total, square, count = lax.psum((total, square, local_count), 'bn')]
  transfers between devices with their start and end apart: 2 -> 0, of which waited for: 1 -> 0; matrix products, arithmetic and copies ran while one was open for 10% -> 0% of each run, Pallas kernels for 0% -> 0%
where the time goes in v1:
time: 292 us; the launch traced here: 291 us
  Pallas kernels  270 us (92%)
  local copies, waits for them, and re-layouts  19 us (7%)
    pallas_call x1, Pallas kernels, grads(): pl.pallas_call(functools.partial(grads_kernel, dims), out_shape=out, in_s...  209 us
    pallas_call x1, Pallas kernels, chain(): pl.pallas_call(functools.partial(chain_kernel, dims), out_shape=out, in_s...  60.9 us

profile of v1, /device:TPU:0, one launch (start us, length us, event | category | flops | bytes accessed | tf_op | source)
XLA Modules:
  0.0 291.0 jit_solution(17885518037109585139)
XLA Ops:
  1.9 60.9 %chain.1 = (f32[2888,128]{1,0:T(8,128)}, f32[4,256,384]{2,1,0:T(8,128)}, f32[4,256,384]{2,1,0:T(8,128)}, f32[256,384]{1,0:T(8,128)}, f32[256,384]{1,0:T(8,128)},...) custom-call(s32[1]{0:T(128)S(6)} %copy.35.count_ref, ...), custom_call_target="tpu_custom_call" | custom-call | tf_op jit(solution)/shard_map/chain/pallas_call | solution.py:428
  62.9 209.1 %grads.1 = (f32[5776,128]{1,0:T(8,128)}, f32[19,64,1024]{2,1,0:T(8,128)}, f32[48,128]{1,0:T(8,128)}, f32[2,4,256,384]{3,2,1,0:T(8,128)}, f32[2,256,384]{2,1,0:T(8,128)}) custom-call(f32[4,256,384]{2,1,0:T(8,128)} %get-tuple-element.30.eo_hbm, f32[4,256,384]{2,1,0:T(8,128)} %get-tuple-element.31.ex_hbm, f32[256,384]{1,0:T(8,128)} %get-tuple-element.32.ao_hbm, ...), custom_call_target="tpu_custom_call" | custom-call | tf_op jit(solution)/shard_map/grads/pallas_call | solution.py:849
  271.9 3.4 %slice.32 = f32[9,64,1024]{2,1,0:T(8,128)} slice(f32[19,64,1024]{2,1,0:T(8,128)} %get-tuple-element.46), slice={[5:14], [0:64], [0:1024]} | slice | bytes 4718592 | tf_op jit(solution)/shard_map/slice | solution.py:878
  275.3 2.1 fusion
  277.4 0.8 fusion.1
  278.2 1.7 slice_bitcast_fusion
  279.9 1.4 slice.37
  281.3 1.1 reshape.70
  282.5 0.3 copy.32
  282.8 0.5 reshape.71
  283.3 1.1 slice.43
  284.5 0.0 copy-start
  284.5 1.4 constant_dynamic-slice_fusion
  285.9 3.5 %copy.37 = f32[1,19,19,1024]{3,0,2,1:T(1,128)} copy(f32[1,19,19,1024]{3,0,2,1:T(1,128)} %bitcast.43) | data formatting | bytes 2957312
  289.4 0.0 copy-done
  289.4 1.6 copy.38
Async XLA Ops:
  284.5 4.9 %copy-start = (f32[5776,128]{1,0:T(8,128)S(1)}, f32[5776,128]{1,0:T(8,128)}, u32[]{:S(2)}) copy-start(f32[5776,128]{1,0:T(8,128)} %get-tuple-element.45) | copy-start | bytes 8871940

commit v2 on v1

--- a/solution.py
+++ b/solution.py
@@ -40,18 +40,15 @@
     return pl.ds(pl.multiple_of(j * size, size), size)
 
 
-def share_order(n_dp):
-    bits = [b for b in range(n_dp.bit_length() - 1)]
-    if len(bits) < 2:
-        return bits
-    return [1, 0] + bits[:1:-1]
-
-
-def share_place(share, n_dp):
+def share_place(share, bits):
     place = 0
-    for bit in share_order(n_dp):
+    for bit in bits:
         place = 2 * place + (share >> bit) % 2
     return place
+
+
+def rest_bits(n_dp):
+    return list(range(n_dp.bit_length() - 2, 1, -1))
 
 
 def flip(index, bit):
@@ -74,8 +71,9 @@
     share = cin // n_dp
     dp, bn = lax.axis_index("dp"), lax.axis_index("bn")
     others = [(dp, lax.rem(bn + k, n_bn)) for k in range(1, n_bn)]
-    pair = (flip(dp, 1)[0], bn)
-    act_bit = flip(dp, 1)[1]
+    pair, pair_bit = (flip(dp, 1)[0], bn), flip(dp, 1)[1]
+    next_, next_bit = (flip(dp, 0)[0], bn), flip(dp, 0)[1]
+    pair_bits, next_bits = [1, 0] + rest_bits(n_dp), [0, 1] + rest_bits(n_dp)
 
     loads = [
         pltpu.make_async_copy(src, dst, wsem.at[k])
@@ -88,7 +86,7 @@
         load.start()
 
     barrier = pltpu.get_barrier_semaphore()
-    for target in others + [pair]:
+    for target in others + [pair, next_]:
         pl.semaphore_signal(barrier, inc=1, device_id=target, device_id_type=MESH)
 
     places = lax.broadcasted_iota(jnp.int32, (rows, LANES), 0)
@@ -229,21 +227,21 @@
 
     matmul_stats(0, taps, ws, z0, width)
     msg[0, 2 * wide_tiles : 2 * wide_tiles + 8, :] = jnp.zeros((8, LANES), F32) + jnp.sum(mask[...], axis=0, keepdims=True)
-    pl.semaphore_wait(barrier, n_bn)
+    pl.semaphore_wait(barrier, n_bn + 1)
     copies = send(0)
 
     def turn_phase(p, _):
         for k in range(cin // LANES):
             block = phases[p, LEAD : LEAD + rows, k * LANES : (k + 1) * LANES].T
             for s in range(k * LANES // share, (k + 1) * LANES // share):
-                at = share_place(s, n_dp) * share
+                at = share_place(s, pair_bits) * share
                 inside = s * share - k * LANES
                 et[p, at : at + share, :] = block[inside : inside + share, :]
         return 0
     lax.fori_loop(0, 4, turn_phase, 0)
     part = cin // 2
-    mine = pl.ds(pl.multiple_of(act_bit * part, part), part)
-    theirs = pl.ds(pl.multiple_of((1 - act_bit) * part, part), part)
+    mine = pl.ds(pl.multiple_of(pair_bit * part, part), part)
+    theirs = pl.ds(pl.multiple_of((1 - pair_bit) * part, part), part)
     keep_e = pltpu.make_async_copy(et.at[0:4, mine, :], eo_hbm, esem.at[0])
     give_e = pltpu.make_async_remote_copy(
         src_ref=et.at[0:4, theirs, :], dst_ref=ex_hbm, send_sem=esem.at[1], recv_sem=esem.at[2],
@@ -293,13 +291,15 @@
     for k in range(half // LANES):
         block = apad[LEAD : LEAD + rows, k * LANES : (k + 1) * LANES].T
         for s in range(k * LANES // share, (k + 1) * LANES // share):
-            at = share_place(s, n_dp) * share
+            at = share_place(s, next_bits) * share
             inside = s * share - k * LANES
             et[4, at : at + share, :] = block[inside : inside + share, :]
-    keep_a = pltpu.make_async_copy(et.at[4, mine, :], ao_hbm, esem.at[3])
+    mine_a = pl.ds(pl.multiple_of(next_bit * part, part), part)
+    theirs_a = pl.ds(pl.multiple_of((1 - next_bit) * part, part), part)
+    keep_a = pltpu.make_async_copy(et.at[4, mine_a, :], ao_hbm, esem.at[3])
     give_a = pltpu.make_async_remote_copy(
-        src_ref=et.at[4, theirs, :], dst_ref=ax_hbm, send_sem=esem.at[4], recv_sem=esem.at[5],
-        device_id=pair, device_id_type=MESH)
+        src_ref=et.at[4, theirs_a, :], dst_ref=ax_hbm, send_sem=esem.at[4], recv_sem=esem.at[5],
+        device_id=next_, device_id_type=MESH)
     keep_a.start()
     give_a.start()
     set_stat(2, receive(2, copies), count, t2, half_tiles)
@@ -436,30 +436,122 @@
     )(count, size, images, cot, ws, wm, wsd, wr, w2, wt, wmg, aff)
 
 
-N_SPATIAL, N_STEM, N_DENSE = 5, 9, 5
+TAPS = 9
+UNITS = ["S%d" % k for k in range(5)] + ["T%d%d" % (k, h) for h in range(2) for k in range(TAPS)] + ["B%d" % k for k in range(6)]
+ORDERS = {}
+for order, names in (
+    ("y12x", ["B0"]),
+    ("y1x2", ["B1", "B3"]),
+    ("xy21", ["B2", "B5"]),
+    ("yx21", ["B4"]),
+    ("x12", ["S0", "S1", "S2", "S3", "S4"]),
+    ("xy2", ["T00", "T01", "T10", "T11", "T21", "T51"]),
+    ("yx2", ["T20", "T31", "T40", "T41", "T50", "T60", "T61", "T70", "T71", "T80", "T81"]),
+    ("y2x", ["T30"]),
+):
+    for name in names:
+        ORDERS[name] = order
+TOKENS = [
+    "B2", "B5", "B2", "B4", "B5", "B0", "B1", "B3", "B2", "B4", "B0", "PS", "S1", "B1", "B2", "B3", "S2", "B5",
+    "PT", "P0", "T10", "S1", "S3", "T00", "B4", "I", "S2", "I", "I", "T10", "I", "B2", "P1", "T01", "S1", "T21",
+    "S3", "I", "S2", "B2", "B0", "T00", "S1", "T51", "I", "I", "S3", "S0", "S2", "B4", "I", "I", "T01", "B1",
+    "T11", "B0", "B2", "S3", "T21", "S1", "B2", "T20", "S1", "S4", "T51", "B3", "B4", "T30", "T71", "B5", "S0",
+    "T10", "S2", "B1", "T60", "S2", "T00", "T01", "T11", "B0", "T21", "S3", "T50", "S3", "B3", "T20", "S4", "B4",
+    "T70", "T51", "B1", "B5", "T80", "B0", "T30", "B3", "S0", "T10", "T71", "T20", "T81", "T00", "B4", "T01",
+    "T60", "B0", "B4", "T61", "T10", "T21", "B0", "T71", "T11", "T00", "T10", "T51", "T01", "T50", "S4", "T00",
+    "T41", "T01", "T21", "B1", "T51", "T60", "T70", "T21", "B5", "T50", "T51", "T40", "T30", "B1", "T80", "T31",
+    "B3", "B1", "T70", "B5", "T81", "T30", "S0", "B5", "T80", "T20", "B3", "T61", "T71", "T81", "B3", "T30",
+    "T11", "T41", "S0", "T30", "S4", "T20", "T60", "S0", "T61", "T20", "T40", "T71", "T50", "T11", "T70", "T71",
+    "T41", "T11", "T31", "S4", "T80", "T60", "T81", "S4", "T40", "T60", "T50", "T61", "T70", "T50", "T41", "T31",
+    "T70", "T80", "T40", "T81", "T61", "T80", "T31", "T81", "T41", "T40", "T61", "T41", "T31", "T40", "T31"
+]
+
+
+class Unit:
+    def __init__(self, name, dims):
+        grid, cin, width, half, n_dp, n_bn = dims
+        self.name, self.kind = name, name[0]
+        order = ORDERS.get(name, {"S": "1x2", "T": "yx2", "B": "xy12"}[self.kind])
+        self.steps = []
+        for letter in order:
+            self.steps += {"x": ["x"], "y": [0], "1": [1], "2": rest_bits(n_dp)}[letter]
+        self.bits = [step for step in self.steps if step != "x"]
+        narrow = name in ("S4", "B2", "B3") or self.kind == "T"
+        rows, cols = (cin if self.kind == "B" else cin // 2), (width // 4 if narrow else width // 2)
+        self.start = (rows, cols)
+        self.pool = self.kind + ("n" if narrow and self.kind == "B" else "")
+        self.shapes = [(rows, cols)] if self.kind == "B" else []
+        for step in self.steps:
+            rows, cols = (rows, cols // 2) if step == "x" else (rows // 2, cols)
+            self.shapes.append((rows, cols))
+        self.final = (rows, cols)
+        self.n_moves = len(self.shapes)
+        self.n_stages = self.n_moves + 3
+
+
+def plan(dims):
+    units = {name: Unit(name, dims) for name in UNITS}
+    shapes, message = {}, 0
+    for unit in units.values():
+        unit.at = []
+        for shape in unit.shapes:
+            unit.at.append((shape, shapes.get(shape, 0)))
+            shapes[shape] = shapes.get(shape, 0) + 1
+        unit.message = message
+        message += unit.n_moves + 3
+    tokens = list(TOKENS)
+    stage = {name: tokens.count(name) for name in UNITS}
+    if not tokens:
+        tokens = ["B%d" % k for k in range(6) for unused in range(2)] + ["PS"] + ["S%d" % k for k in range(5)] + ["PT", "P0", "P1"]
+        tokens += [t for k in range(TAPS) for t in ("T%d0" % k, "T%d1" % k, "I")]
+        stage = {name: tokens.count(name) for name in UNITS}
+    while any(stage[name] < units[name].n_stages for name in UNITS):
+        for name in UNITS:
+            if stage[name] < units[name].n_stages:
+                tokens.append(name)
+                stage[name] += 1
+    kinds = ("S", "T", "B", "Bn")
+    seen, count, free = {}, {kind: 0 for kind in kinds}, {kind: [] for kind in kinds}
+    for token in tokens:
+        if token in units:
+            unit = units[token]
+            k = seen.get(token, 0)
+            seen[token] = k + 1
+            if k == 0:
+                if not free[unit.pool]:
+                    free[unit.pool].append(count[unit.pool])
+                    count[unit.pool] += 1
+                unit.slot = free[unit.pool].pop(0)
+            elif k == 1:
+                free[unit.pool].append(unit.slot)
+    return units, shapes, message, tokens, count
 
 
 def grads_kernel(
     dims,
     eo_hbm, ex_hbm, ao_hbm, ax_hbm, g0_hbm, g2_hbm,
     stem_hbm, joined_hbm, main_hbm, res_hbm, merge_hbm, tside_hbm, red_hbm, mside_hbm, sums_ref, ws_hbm,
-    igrad_ref, out_hbm, total_ref, ec_hbm, ac_hbm,
-    g0r, g2r, at_land, at_cat, et_land, et_cat, units, cuts_a, last_a, cuts_b, pair_b, cross_b, own_g, sums_in,
-    load_sem, give_sem, take_sem, a_send, a_recv, b_send, b_recv, out_sem, s_send, s_recv,
+    igrad_hbm, out_stem, out_spatial, out_merge, out_transit, out_reduce, out_split, total_ref,
+    g0r, g2r, landed, own_g, sums_in, at_land, at_cat, et_land, spatial,
+    load_sem, give_sem, take_sem, m_send, m_recv, keep_sem, s_send, s_recv,
 ):
     grid, cin, width, half, n_dp, n_bn = dims
+    units, shapes, n_messages, tokens, pool = plan(dims)
+    shape_list = list(shapes)
     pitch = grid + 1
-    rows = at_cat.shape[1] // 4
+    rows = own_g.shape[0] - LEAD
     share = cin // n_dp
     part = cin // 2
+    quarter = width // 4
     dp, bn = lax.axis_index("dp"), lax.axis_index("bn")
-    order = share_order(n_dp)
-    order_a = order[1:]
+    n_bits = n_dp.bit_length() - 1
     sib, core = flip(bn, 0)
     over, cross = flip(bn, 1)
-    act_dp, act_bit = flip(dp, 1)
-    partners = [(dp, sib), (dp, over), (act_dp, bn), (act_dp, sib)] + [(flip(dp, b)[0], bn) for b in order_a]
-    bit_of = {b: flip(dp, b) for b in order}
+    bit_of = [flip(dp, b) for b in range(n_bits)]
+    sibling, across = (dp, sib), (dp, over)
+    along = [(bit_of[b][0], bn) for b in range(n_bits)]
+    next_sib, pair_sib = (bit_of[0][0], sib), (bit_of[1][0], sib)
+    partners = [sibling, across, next_sib, pair_sib] + along
 
     barrier = pltpu.get_barrier_semaphore()
     for target in partners:
@@ -470,391 +562,421 @@
         return pltpu.make_async_remote_copy(
             src_ref=src, dst_ref=dst, send_sem=send, recv_sem=recv, device_id=target, device_id_type=MESH)
 
-    half2, half0 = half // 2, width // 2
-
-    def cols(which, size):
+    def part_of(which, size):
         return pl.ds(pl.multiple_of(which * size, size), size)
 
-    gives = []
-    fields = ((g2_hbm, g2r, half2), (g0_hbm, g0r, half0))
-    for f, (src, dst, size) in enumerate(fields):
-        lead = LEAD if f == 0 else 0
-        for k, (target, which) in enumerate((((dp, sib), 1 - core), ((act_dp, bn), core), ((act_dp, sib), 1 - core))):
+    half2 = half // 2
+    gives, locals_ = [], []
+    for k, (target, which) in enumerate(((sibling, 1 - core), (along[0], core), (next_sib, 1 - core))):
+        gives.append(remote(
+            g2_hbm.at[:, part_of(which, half2)], g2r.at[k + 1, pl.ds(LEAD, rows)], give_sem.at[k], take_sem.at[k], target))
+    for h in range(2):
+        for k, (target, which) in enumerate(((sibling, 1 - core), (along[1], core), (pair_sib, 1 - core))):
+            n = 3 + 3 * h + k
             gives.append(remote(
-                src.at[:, cols(which, size)], dst.at[k + 1, pl.ds(lead, rows)],
-                give_sem.at[3 * f + k], take_sem.at[3 * f + k], target))
+                g0_hbm.at[:, part_of(2 * which + h, quarter)], g0r.at[h, k + 1, pl.ds(0, rows)],
+                give_sem.at[n], take_sem.at[n], target))
     forwards = [
-        remote(ao_hbm, ac_hbm.at[0], give_sem.at[6], take_sem.at[6], (dp, sib)),
-        remote(ax_hbm, ac_hbm.at[1], give_sem.at[7], take_sem.at[7], (dp, sib)),
-        remote(eo_hbm, ec_hbm.at[0], give_sem.at[8], take_sem.at[8], (dp, sib)),
-        remote(ex_hbm, ec_hbm.at[1], give_sem.at[9], take_sem.at[9], (dp, sib)),
+        remote(land.at[n], land.at[n + 2], give_sem.at[9 + k], take_sem.at[9 + k], sibling)
+        for k, (land, n) in enumerate(((at_land, 0), (at_land, 1), (et_land, 0), (et_land, 1)))
     ]
+    own_parts = [
+        pltpu.make_async_copy(src, land, load_sem.at[11 + k])
+        for k, (src, land) in enumerate(
+            ((ao_hbm, at_land.at[0]), (ax_hbm, at_land.at[1]), (eo_hbm, et_land.at[0]), (ex_hbm, et_land.at[1])))
+    ]
+    for load in own_parts:
+        load.start()
+    for n in range(3):
+        gives[n].start()
+    for n in (3, 4, 5):
+        gives[n].start()
+    for n in (6, 7, 8):
+        gives[n].start()
     locals_ = [
-        pltpu.make_async_copy(g2_hbm.at[:, cols(core, half2)], g2r.at[0, pl.ds(LEAD, rows)], load_sem.at[0]),
-        pltpu.make_async_copy(g0_hbm.at[:, cols(core, half0)], g0r.at[0, pl.ds(0, rows)], load_sem.at[1]),
-        pltpu.make_async_copy(g0_hbm, own_g.at[pl.ds(0, rows)], load_sem.at[2]),
-        pltpu.make_async_copy(ao_hbm, at_land.at[0], load_sem.at[3]),
-        pltpu.make_async_copy(ax_hbm, at_land.at[1], load_sem.at[4]),
+        pltpu.make_async_copy(g2_hbm.at[:, part_of(core, half2)], g2r.at[0, pl.ds(LEAD, rows)], load_sem.at[0]),
+        pltpu.make_async_copy(g0_hbm.at[:, part_of(2 * core, quarter)], g0r.at[0, 0, pl.ds(0, rows)], load_sem.at[1]),
+        pltpu.make_async_copy(g0_hbm.at[:, part_of(2 * core + 1, quarter)], g0r.at[1, 0, pl.ds(0, rows)], load_sem.at[2]),
+        pltpu.make_async_copy(g0_hbm, own_g.at[pl.ds(0, rows)], load_sem.at[3]),
     ]
-    for k in (0, 1, 2):
-        gives[k].start()
-    forwards[0].start()
-    forwards[1].start()
-    for k in (3, 4, 5):
-        gives[k].start()
-    forwards[2].start()
-    forwards[3].start()
     for load in locals_:
         load.start()
+    for load, forward in zip(own_parts, forwards):
+        load.wait()
+        forward.start()
 
     def sums_step(k):
-        return remote(total_ref if k else sums_ref, sums_in.at[k], s_send.at[k], s_recv.at[k], (bit_of[order[k]][0], bn))
-
-    def sums_next(k):
-        sums_step(k).wait()
-        total_ref[...] = (total_ref[...] if k else sums_ref[...]) + sums_in[k]
-        if k + 1 < len(order):
-            sums_step(k + 1).start()
+        return remote(total_ref if k else sums_ref, sums_in.at[k], s_send.at[k], s_recv.at[k], along[k])
+
+    sums_done = []
+
+    def sums_next():
+        k = len(sums_done)
+        if k < n_bits:
+            sums_done.append(k)
+            sums_step(k).wait()
+            total_ref[...] = (total_ref[...] if k else sums_ref[...]) + sums_in[k]
+            if k + 1 < n_bits:
+                sums_step(k + 1).start()
     sums_step(0).start()
 
     for k in range(4):
         g2r[k, 0:LEAD, :] = jnp.zeros((LEAD, half2), F32)
         g2r[k, LEAD + rows :, :] = jnp.zeros((LEAD, half2), F32)
-        g0r[k, rows:, :] = jnp.zeros((LEAD, half0), F32)
+        for h in range(2):
+            g0r[h, k, rows:, :] = jnp.zeros((LEAD, quarter), F32)
     own_g[rows:, :] = jnp.zeros((LEAD, width), F32)
 
-    n_b = len(order)
-
-    def b_core(u, full):
-        return remote(full.at[u % 2, :, cols(1 - core, half0)], pair_b.at[u], b_send.at[0, u], b_recv.at[0, u], (dp, sib))
-
-    def b_cross(u):
-        return remote(pair_b.at[u, :, cols(1 - cross, 256)], cross_b.at[u], b_send.at[1, u], b_recv.at[1, u], (dp, over))
-
-    def b_step(u, i):
-        src = cross_b if i == 0 else cuts_b[i - 1]
-        size = cuts_b[i].shape[1]
-        partner, bit = bit_of[order[i]]
-        at = pl.ds(pl.multiple_of((1 - bit) * size, size), size)
-        return remote(src.at[u, at], cuts_b[i].at[u], b_send.at[2 + i, u], b_recv.at[2 + i, u], (partner, bn))
-
-    def add_rows(dst, src, size):
+    local = {}
+
+    def landing(unit, k):
+        shape, n = unit.at[k]
+        return landed[shape_list.index(shape)].at[n]
+
+    def source(unit, k):
+        return local[unit.kind](unit) if k == 0 else landing(unit, k - 1)
+
+    def move_of(unit, k):
+        size_r, size_c = unit.shapes[k]
+        step = "c" if unit.kind == "B" and k == 0 else unit.steps[k - (unit.kind == "B")]
+        if step == "c":
+            return sibling, (pl.ds(0, size_r), part_of(1 - core, size_c)), (None, part_of(core, size_c))
+        if step == "x":
+            return across, (pl.ds(0, size_r), part_of(1 - cross, size_c)), (None, part_of(cross, size_c))
+        bit = bit_of[step][1]
+        return along[step], (part_of(1 - bit, size_r), pl.ds(0, size_c)), (bit, pl.ds(0, size_c))
+
+    def move(unit, k):
+        target, gone, unused = move_of(unit, k)
+        m = unit.message + k
+        return remote(source(unit, k).at[gone[0], gone[1]], landing(unit, k), m_send.at[m], m_recv.at[m], target)
+
+    def add_own(unit, k):
+        unused, unused2, (bit, columns) = move_of(unit, k)
+        size = unit.shapes[k][0]
+        src, dst = source(unit, k), landing(unit, k)
         n = min(size, 64)
 
-        def body(k, _):
-            r = pl.ds(pl.multiple_of(k * n, n), n)
-            dst(r)
+        def body(i, _):
+            r = pl.ds(pl.multiple_of(i * n, n), n)
+            own = r if bit is None else pl.ds(pl.multiple_of(bit * size + i * n, 8), n)
+            dst[r, :] = dst[r, :] + src[own, columns]
             return 0
         lax.fori_loop(0, size // n, body, 0)
 
-    def b_after_core(u, full):
-        b_core(u, full).wait()
-
-        def add(r):
-            pair_b[u, r, :] = pair_b[u, r, :] + full[u % 2, r, cols(core, half0)]
-        add_rows(add, None, cin)
-        b_cross(u).start()
-
-    def b_after(u, i):
-        if i == 0:
-            b_cross(u).wait()
-
-            def add(r):
-                cross_b[u, r, :] = cross_b[u, r, :] + pair_b[u, r, cols(cross, 256)]
-            add_rows(add, None, cin)
+    def pieces(unit):
+        name = unit.name
+        cols = unit.final[1]
+        k = int(name[1])
+        at = 2 * core + cross
+        if unit.kind == "T":
+            h = int(name[2])
+            base = pl.multiple_of(core * (width // 2) + h * quarter, quarter)
+            mine = out_stem.at[k, :, pl.ds(pl.multiple_of(base + cross * cols, cols), cols)]
+            return [(mine, 0)], out_stem.at[k, :, pl.ds(base, quarter)]
+        if unit.kind == "S":
+            mine = [(out_spatial.at[t, :, part_of(at, half // 4)], (t - 2 * k) * (half // 4)) for t in range(2 * k, min(2 * k + 2, TAPS))]
+            return mine, out_spatial.at[pl.ds(2 * k, len(mine)), :, part_of(core, half2)]
+        if k < 2:
+            r = pl.ds(k * share, share)
+            return [(out_merge.at[r, part_of(at, quarter)], 0)], out_merge.at[r, part_of(core, width // 2)]
+        if k < 4:
+            out = out_transit if k == 2 else out_reduce
+            return [(out.at[:, part_of(at, half // 4)], 0)], out.at[:, part_of(core, half2)]
+        r = pl.ds((k - 4) * share, share)
+        return [(out_split.at[core, r, part_of(cross, half2)], 0)], out_split.at[core, r, :]
+
+    def gather_cross(unit):
+        m = unit.message + unit.n_moves
+        copies = []
+        mine, unused = pieces(unit)
+        final = landing(unit, unit.n_moves - 1)
+        for n, (place, col) in enumerate(mine):
+            src = final.at[:, pl.ds(col, place.shape[-1])]
+            copies.append(pltpu.make_async_copy(src, place, keep_sem.at[m + n]))
+            copies.append(remote(src, place, m_send.at[m + n], m_recv.at[m + n], across))
+        return copies
+
+    def gather_core(unit):
+        m = unit.message + unit.n_moves + 2
+        both = pieces(unit)[1]
+        return remote(both, both, m_send.at[m], m_recv.at[m], sibling)
+
+    stage = {name: 0 for name in units}
+
+    def advance(name, compute):
+        unit = units[name]
+        k = stage[name]
+        stage[name] = k + 1
+        if k == 0:
+            compute(unit)
+            move(unit, 0).start()
+        elif k <= unit.n_moves:
+            move(unit, k - 1).wait()
+            add_own(unit, k - 1)
+            if k < unit.n_moves:
+                move(unit, k).start()
+            else:
+                for copy in gather_cross(unit):
+                    copy.start()
+        elif k == unit.n_moves + 1:
+            for copy in gather_cross(unit):
+                copy.wait()
+            gather_core(unit).start()
         else:
-            b_step(u, i - 1).wait()
-            src = cross_b if i == 1 else cuts_b[i - 2]
-            dst = cuts_b[i - 1]
-            size = dst.shape[1]
-            bit = bit_of[order[i - 1]][1]
-
-            def add(r):
-                at = pl.ds(pl.multiple_of(bit * size + r.start, 8), r.size)
-                dst[u, r, :] = dst[u, r, :] + src[u, at, :]
-            add_rows(add, None, size)
-        if i < n_b:
-            b_step(u, i).start()
-
-    def place(at):
-        return cols(2 * core + at, 256)
-
-    def gather_cross(u, src):
-        mine = out_hbm.at[u, :, place(cross)]
-        return (
-            pltpu.make_async_copy(src, mine, out_sem.at[0, u]),
-            remote(src, mine, out_sem.at[1, u], out_sem.at[2, u], (dp, over)),
-        )
-
-    def gather_core(u):
-        both = out_hbm.at[u, :, cols(core, half0)]
-        return remote(both, both, out_sem.at[3, u], out_sem.at[4, u], (dp, sib))
-
-    def dense_phase(full, turned, r_merge, r_tside, r_red, r_mside, land):
-        ins = ((joined_hbm, land, 2), (res_hbm, land, 1), (main_hbm, land, 1), (stem_hbm, land, 2))
+            gather_core(unit).wait()
+
+    local["S"] = lambda unit: spatial.at[unit.slot]
+
+    def prepare_spatial():
+        for n in range(2):
+            forwards[n].wait()
+        for k in range(3):
+            gives[k].wait()
+        locals_[0].wait()
+        for slot, n in enumerate((0, 2, 1, 3)):
+            at_cat[:, slot * rows : (slot + 1) * rows] = at_land[n].astype(BF16)
+        sums_next()
+
+    def compute_spatial(unit):
+        k = int(unit.name[1])
+        dst = local["S"](unit)
+        c = unit.start[1] // 2
+        for h in range(2):
+            t = 2 * k + h
+            if t < TAPS:
+                off = LEAD - pitch * (t // 3 - 1) - (t % 3 - 1)
+                right = jnp.concatenate([g2r[s, off : off + rows, :].astype(BF16) for s in range(4)], axis=0)
+                value = dot(at_cat[...], right)
+                for x in range(2):
+                    dst[:, c * x + LANES * h : c * x + LANES * (h + 1)] = value[:, LANES * x : LANES * (x + 1)]
+
+    cut = tokens.index("PT")
+
+    def dense_phase(full, narrow, turned, r_merge, r_tside, r_red, r_mside, land):
         rights = [pltpu.make_async_copy(s, d, load_sem.at[5 + k]) for k, (s, d) in enumerate(
             ((merge_hbm, r_merge), (tside_hbm, r_tside), (red_hbm, r_red), (mside_hbm, r_mside)))]
+        lefts = [(joined_hbm, 0, 2), (res_hbm, 2, 1), (main_hbm, 3, 1), (stem_hbm, 4, 2)]
+        loads = [
+            pltpu.make_async_copy(src, land.at[n % 2, :, pl.ds(0, parts * half)], load_sem.at[9 + n % 2])
+            for n, (src, first, parts) in enumerate(lefts)]
+        loads[0].start()
         for load in rights:
             load.start()
-
-        def turn(src, first, parts):
-            size = parts * half
-            load = pltpu.make_async_copy(src, land.at[:, pl.ds(0, size)], load_sem.at[9])
-            load.start()
-            load.wait()
-            for k in range(size // LANES):
-                block = land[:, k * LANES : (k + 1) * LANES].astype(F32).T
+        loads[1].start()
+        done = set()
+        local["B"] = lambda unit: (full if unit.pool == "B" else narrow).at[unit.slot]
+
+        def turn(n):
+            src, first, parts = lefts[n]
+            loads[n].wait()
+            for k in range(parts * half // LANES):
+                block = land[n % 2, :, k * LANES : (k + 1) * LANES].astype(F32).T
                 for piece in range(LANES // share):
                     row = k * LANES + piece * share
                     s, h = (row // share) // parts, (row // share) % parts
-                    at = share_place(s, n_dp) * share
+                    at = share_place(s, units["B%d" % (first + h)].bits) * share
                     turned[first + h, at : at + share, :] = block[piece * share : (piece + 1) * share].astype(BF16)
-
-        def fill(u, left, right_ref, lo, hi):
-            for n in range((hi - lo) // 256):
-                full[u % 2, :, pl.ds(lo + n * 256, 256)] = dot(turned[left], right_ref[:, pl.ds(lo_of(right_ref, lo) + n * 256, 256)])
-
-        def lo_of(ref, lo):
-            return lo if ref.shape[1] >= width else 0
-
-        turn(joined_hbm, 0, 2)
-        rights[0].wait()
-        fill(0, 0, r_merge, 0, width)
-        b_core(0, full).start()
-        fill(1, 1, r_merge, 0, width)
-        b_core(1, full).start()
-        turn(res_hbm, 2, 1)
-        turn(main_hbm, 3, 1)
-        b_after_core(0, full)
-        rights[1].wait()
-        rights[2].wait()
-        fill(2, 2, r_tside, 0, half)
-        fill(2, 3, r_red, half, 2 * half)
-        b_core(2, full).start()
-        b_after_core(1, full)
-        turn(stem_hbm, 4, 2)
-        rights[3].wait()
-        fill(3, 4, r_mside, 0, width)
-        b_core(3, full).start()
-        b_after_core(2, full)
-        fill(4, 5, r_mside, 0, width)
-        b_core(4, full).start()
-        b_after_core(3, full)
-        b_after_core(4, full)
+            if n + 2 < len(loads):
+                loads[n + 2].start()
+
+        def compute(unit):
+            if unit.kind == "S":
+                return compute_spatial(unit)
+            k = int(unit.name[1])
+            for m in range({0: 0, 1: 0, 2: 1, 3: 2, 4: 3, 5: 3}[k] + 1):
+                if m not in done:
+                    turn(m)
+                    done.add(m)
+            right, r = [(r_merge, 0), (r_merge, 0), (r_tside, 1), (r_red, 2), (r_mside, 3), (r_mside, 3)][k]
+            if ("right", r) not in done:
+                rights[r].wait()
+                done.add(("right", r))
+            dst = local["B"](unit)
+            for n in range(2 * unit.start[1] // 256):
+                c = pl.ds(n * 256, 256)
+                dst[:, c] = dot(turned[k], right[:, c])
+
+        for token in tokens[:cut]:
+            if token == "PS":
+                prepare_spatial()
+            elif token in units:
+                advance(token, compute)
+        for name in units:
+            while units[name].kind == "B" and stage[name] < 2:
+                advance(name, compute)
 
     pl.run_scoped(
-        dense_phase, pltpu.VMEM((2, cin, width), F32), pltpu.VMEM((6, cin, rows), BF16),
+        dense_phase,
+        pltpu.VMEM((pool["B"], cin, width), F32), pltpu.VMEM((pool["Bn"], cin, half), F32), pltpu.VMEM((6, cin, rows), BF16),
         pltpu.VMEM((rows, width), BF16), pltpu.VMEM((rows, 2 * half), BF16), pltpu.VMEM((rows, half), BF16),
-        pltpu.VMEM((rows, 2 * half), BF16), pltpu.VMEM((rows, width), BF16))
-
-    n_a = len(order_a)
-    n_units = N_SPATIAL + N_STEM
-
-    def a_step(u, i):
-        src = units.at[lax.rem(u, 3)] if i == 0 else cuts_a[i - 1].at[u]
-        size = cuts_a[i].shape[1]
-        partner, bit = bit_of[order_a[i]]
-        at = pl.ds(pl.multiple_of((1 - bit) * size, size), size)
-        return remote(src.at[at], cuts_a[i].at[u], a_send.at[i, u], a_recv.at[i, u], (partner, bn))
-
-    def a_cross(u):
-        return remote(cuts_a[-1].at[u, :, cols(1 - cross, 256)], last_a.at[u], a_send.at[n_a, u], a_recv.at[n_a, u], (dp, over))
-
-    def a_after(u, i):
-        if i < n_a:
-            a_step(u, i).wait()
-            dst = cuts_a[i]
-            size = dst.shape[1]
-            bit = bit_of[order_a[i]][1]
-
-            def add(r):
-                at = pl.ds(pl.multiple_of(bit * size + r.start, 8), r.size)
-                own = units[lax.rem(u, 3), at, :] if i == 0 else cuts_a[i - 1][u, at, :]
-                dst[u, r, :] = dst[u, r, :] + own
-            add_rows(add, None, size)
-            if i + 1 < n_a:
-                a_step(u, i + 1).start()
-            else:
-                a_cross(u).start()
-        elif i == n_a:
-            a_cross(u).wait()
-            last_a[u] = last_a[u] + cuts_a[-1][u, :, cols(cross, 256)]
-            for copy in gather_cross(u, last_a.at[u]):
-                copy.start()
-        elif i == n_a + 1:
-            for copy in gather_cross(u, last_a.at[u]):
-                copy.wait()
-            gather_core(u).start()
-        else:
-            gather_core(u).wait()
-
-    n_stage = n_a + 3
-
-    def advance(t, known):
-        for i in range(n_stage):
-            if isinstance(t, int):
-                if 0 <= t - 1 - i < n_units:
-                    a_after(t - 1 - i, i)
-            elif i + 1 <= known:
-                a_after(t - 1 - i, i)
-            else:
-                @pl.when(t - 1 - i >= 0)
-                def _(i=i):
-                    a_after(t - 1 - i, i)
-
-    for load in locals_:
-        load.wait()
-    for k in (0, 1):
-        forwards[k].wait()
-        load = pltpu.make_async_copy(ac_hbm.at[k], at_land.at[2 + k], load_sem.at[10])
-        load.start()
-        load.wait()
-    for k in (0, 1, 2):
-        gives[k].wait()
-    for slot, land in enumerate((0, 2, 1, 3)):
-        at_cat[:, slot * rows : (slot + 1) * rows] = at_land[land].astype(BF16)
-    sums_next(0)
-    for u in range(N_SPATIAL):
-        for h in range(2):
-            k = 2 * u + h
-            if k < 9:
-                off = LEAD - pitch * (k // 3 - 1) - (k % 3 - 1)
-                right = jnp.concatenate([g2r[s, off : off + rows, :].astype(BF16) for s in range(4)], axis=0)
-                value = dot(at_cat[...], right)
-            else:
-                value = jnp.zeros((part, half2), F32)
-            for x in range(2):
-                units[u % 3, :, 256 * x + LANES * h : 256 * x + LANES * (h + 1)] = value[:, LANES * x : LANES * (x + 1)]
-        a_step(u, 0).start()
-        advance(u, 0)
-    for u in range(N_DENSE):
-        b_after(u, 0)
-    sums_next(1)
-
-    def stem_phase(shifted, own_shift, image, weight, wsem):
-        def load_w(k):
-            return pltpu.make_async_copy(
-                ws_hbm.at[pl.ds(pl.multiple_of(k * cin, cin), cin)], weight.at[lax.rem(k, 2)], wsem.at[lax.rem(k, 2)])
-        load_w(0).start()
-        for k in (2, 3):
-            forwards[k].wait()
-        for p in range(4):
-            pieces = [pltpu.make_async_copy(src, et_land.at[s], load_sem.at[11 + s]) for s, src in enumerate(
-                (eo_hbm.at[p], ec_hbm.at[0, p], ex_hbm.at[p], ec_hbm.at[1, p]))]
-            for piece in pieces:
-                piece.start()
-            for s, piece in enumerate(pieces):
-                piece.wait()
-                et_cat[p, :, s * rows : (s + 1) * rows] = et_land[s].astype(BF16)
-            image[p] = jnp.zeros(image.shape[1:], F32)
-        for sh, off in enumerate((0, 1, pitch, pitch + 1)):
-            own_shift[sh] = own_g[off : off + rows, :].astype(BF16)
-        for k in (3, 4, 5):
-            gives[k].wait()
-        for sh, off in enumerate((0, 1, pitch, pitch + 1)):
-            for s in range(4):
-                shifted[sh, s * rows : (s + 1) * rows, :] = g0r[s, off : off + rows, :].astype(BF16)
-
-        def slot(k, _):
-            a, b = k // 3, lax.rem(k, 3)
-            p = 2 * jnp.where(a == 1, 0, 1) + jnp.where(b == 1, 0, 1)
-            sh = 2 * jnp.where(a == 0, 1, 0) + jnp.where(b == 0, 1, 0)
-            u = N_SPATIAL + k
-            for n in range(half0 // 256):
-                units[lax.rem(u, 3), :, n * 256 : (n + 1) * 256] = dot(et_cat[p], shifted[sh, :, n * 256 : (n + 1) * 256])
-            a_step(u, 0).start()
-
-            @pl.when(k < 8)
-            def _():
-                load_w(k + 1).start()
-            load_w(k).wait()
+        pltpu.VMEM((rows, 2 * half), BF16), pltpu.VMEM((2, rows, width), BF16))
+
+    def stem_phase(shifted, own_shift, image, weight, wsem, et_cat, blocks, igrad):
+        local["T"] = lambda unit: blocks.at[unit.slot]
+        offsets = (0, 1, pitch, pitch + 1)
+        image_taps = [4, 3, 5, 1, 7, 0, 2, 6, 8]
+        done = []
+
+        def tap(k):
+            a, b = k // 3, k % 3
+            return 2 * (a != 1) + (b != 1), 2 * (a == 0) + (b == 0)
+
+        def compute(unit):
+            if unit.kind == "S":
+                return compute_spatial(unit)
+            p, sh = tap(int(unit.name[1]))
+            local["T"](unit)[...] = dot(et_cat[p], shifted[int(unit.name[2]), sh])
+
+        def image_step():
+            k = image_taps[len(done)]
+            p, sh = tap(k)
+            if len(done) + 1 < TAPS:
+                load_w_next = image_taps[len(done) + 1]
+                pltpu.make_async_copy(
+                    ws_hbm.at[pl.ds(load_w_next * cin, cin)], weight.at[(len(done) + 1) % 2], wsem.at[(len(done) + 1) % 2]).start()
+            pltpu.make_async_copy(ws_hbm.at[pl.ds(k * cin, cin)], weight.at[len(done) % 2], wsem.at[len(done) % 2]).wait()
+            first = k in (4, 3, 1, 0)
             for n in range(cin // 256):
                 c = slice(n * 256, (n + 1) * 256)
-                image[p, :, c] = image[p, :, c] + dot_t(own_shift[sh], weight[lax.rem(k, 2), c, :])
-            advance(u, N_SPATIAL)
-            return 0
-
-        lax.fori_loop(0, 3, slot, 0)
-        for u in range(N_DENSE):
-            b_after(u, 1)
-        lax.fori_loop(3, 6, slot, 0)
-        for u in range(N_DENSE):
-            b_after(u, 2)
-        lax.fori_loop(6, 9, slot, 0)
-
-        def spread(p, _):
-            pr, pc = p // 2, lax.rem(p, 2)
-            for r in range(grid):
-                for k in range(cin // LANES):
-                    start = ((2 * r + pr) * 2 * grid + pc) * (cin // LANES) + k
-                    igrad_ref[pl.ds(start, grid, stride=2 * cin // LANES), :] = image[p, r * pitch : r * pitch + grid, k * LANES : (k + 1) * LANES]
-            return 0
-        lax.fori_loop(0, 4, spread, 0)
+                value = dot_t(own_shift[sh], weight[len(done) % 2, c, :])
+                image[:, c] = value if first else image[:, c] + value
+            done.append(k)
+            if k in (4, 5, 7, 8):
+                pr, pc = p // 2, p % 2
+
+                def spread(r, _):
+                    for n in range(cin // LANES):
+                        start = ((2 * r + pr) * 2 * grid + pc) * (cin // LANES) + n
+                        igrad[pl.ds(start, grid, stride=2 * cin // LANES), :] = line_of(r, n)
+                    return 0
+
+                def line_of(r, n):
+                    return image[r * pitch : r * pitch + grid, n * LANES : (n + 1) * LANES]
+                for r in range(grid):
+                    spread(r, 0)
+            if len(done) == TAPS:
+                pltpu.make_async_copy(igrad, igrad_hbm, load_sem.at[15]).start()
+
+        def run(token):
+            if token == "PT":
+                pltpu.make_async_copy(ws_hbm.at[pl.ds(image_taps[0] * cin, cin)], weight.at[0], wsem.at[0]).start()
+                for n in (2, 3):
+                    forwards[n].wait()
+
+                for p in range(4):
+                    for slot, n in enumerate((0, 2, 1, 3)):
+                        et_cat[p, :, slot * rows : (slot + 1) * rows] = et_land[n, p].astype(BF16)
+                locals_[3].wait()
+                for sh, off in enumerate(offsets):
+                    own_shift[sh] = own_g[off : off + rows, :].astype(BF16)
+                sums_next()
+            elif token in ("P0", "P1"):
+                h = int(token[1])
+                for k in range(3):
+                    gives[3 + 3 * h + k].wait()
+                locals_[1 + h].wait()
+                for sh, off in enumerate(offsets):
+                    for s in range(4):
+                        shifted[h, sh, s * rows : (s + 1) * rows, :] = g0r[h, s, off : off + rows, :].astype(BF16)
+                sums_next()
+            elif token == "PS":
+                prepare_spatial()
+            elif token == "I":
+                if len(done) < TAPS:
+                    image_step()
+            elif token in units:
+                advance(token, compute)
+
+        for token in tokens[cut:]:
+            run(token)
+        while len(done) < TAPS:
+            image_step()
+        for k in range(n_bits):
+            sums_next()
+        pltpu.make_async_copy(igrad, igrad_hbm, load_sem.at[15]).wait()
 
     pl.run_scoped(
-        stem_phase, pltpu.VMEM((4, 4 * rows, half0), BF16), pltpu.VMEM((4, rows, width), BF16),
-        pltpu.VMEM((4, rows, cin), F32), pltpu.VMEM((2, cin, width), BF16), pltpu.SemaphoreType.DMA((2,)))
-
-    for i in range(3, n_b + 1):
-        for u in range(N_DENSE):
-            b_after(u, i)
-    for k in range(2, len(order)):
-        sums_next(k)
-    final = cuts_b[-1]
-    for u in range(N_DENSE):
-        for copy in gather_cross(n_units + u, final.at[u]):
-            copy.start()
-    for t in range(n_units, n_units + n_stage):
-        advance(t, 0)
-    for u in range(N_DENSE):
-        for copy in gather_cross(n_units + u, final.at[u]):
-            copy.wait()
-        gather_core(n_units + u).start()
-    for u in range(N_DENSE):
-        gather_core(n_units + u).wait()
+        stem_phase,
+        pltpu.VMEM((2, 4, 4 * rows, quarter), BF16), pltpu.VMEM((4, rows, width), BF16), pltpu.VMEM((rows, cin), F32),
+        pltpu.VMEM((2, cin, width), BF16), pltpu.SemaphoreType.DMA((2,)),
+        pltpu.VMEM((4, part, 4 * rows), BF16),
+        pltpu.VMEM((pool["T"], part, quarter), F32), pltpu.VMEM((4 * grid * grid * (cin // LANES), LANES), F32))
 
 
 def grads(dims, eo, ex, ao, ax, g0, g2, stem_low, joined, main_low, res_low, merge_in, tside, red_in, mside, sums, ws):
     grid, cin, width, half, n_dp, n_bn = dims
+    units, shapes, n_messages, tokens, pool = plan(dims)
     rows = g0.shape[0]
     share = cin // n_dp
     part = cin // 2
-    n_units = N_SPATIAL + N_STEM
     sd = jax.ShapeDtypeStruct
     vm, any_ = pl.BlockSpec(memory_space=pltpu.VMEM), pl.BlockSpec(memory_space=pl.ANY)
-    n_bits = len(share_order(n_dp))
-    half0, half2 = width // 2, half // 2
+    n_bits = n_dp.bit_length() - 1
     dma = pltpu.SemaphoreType.DMA
     scratch = [
-        pltpu.VMEM((4, rows + LEAD, half0), F32), pltpu.VMEM((4, LEAD + rows + LEAD, half2), F32),
-        pltpu.VMEM((4, part, rows), F32), pltpu.VMEM((part, 4 * rows), BF16),
-        pltpu.VMEM((4, part, rows), F32), pltpu.VMEM((4, part, 4 * rows), BF16),
-        pltpu.VMEM((3, part, half0), F32),
-        [pltpu.VMEM((n_units, part >> (i + 1), half0), F32) for i in range(n_bits - 1)],
-        pltpu.VMEM((n_units, share, 256), F32),
-        [pltpu.VMEM((N_DENSE, cin >> (i + 1), 256), F32) for i in range(n_bits)],
-        pltpu.VMEM((N_DENSE, cin, half0), F32), pltpu.VMEM((N_DENSE, cin, 256), F32),
+        pltpu.VMEM((2, 4, rows + LEAD, width // 4), F32), pltpu.VMEM((4, LEAD + rows + LEAD, half // 2), F32),
+        [pltpu.VMEM((n,) + shape, F32) for shape, n in shapes.items()],
         pltpu.VMEM((rows + LEAD, width), F32),
         pltpu.VMEM((n_bits,) + sums.shape, F32),
-        dma((16,)), dma((10,)), dma((10,)),
-        dma((n_bits, n_units)), dma((n_bits, n_units)), dma((n_bits + 2, N_DENSE)), dma((n_bits + 2, N_DENSE)),
-        dma((5, n_units + N_DENSE)), dma((n_bits,)), dma((n_bits,)),
+        pltpu.VMEM((4, part, rows), F32), pltpu.VMEM((part, 4 * rows), BF16), pltpu.VMEM((4, 4, part, rows), F32),
+        pltpu.VMEM((pool["S"], part, width // 2), F32),
+        dma((16,)), dma((13,)), dma((13,)), dma((n_messages,)), dma((n_messages,)), dma((n_messages,)),
+        dma((n_bits,)), dma((n_bits,)),
     ]
     out = (
         sd((4 * grid * grid * (cin // LANES), LANES), F32),
-        sd((n_units + N_DENSE, share, width), F32),
+        sd((TAPS, share, width), F32), sd((TAPS, share, half), F32), sd((2 * share, width), F32),
+        sd((share, half), F32), sd((share, half), F32), sd((2, 2 * share, half), F32),
         sd(sums.shape, F32),
-        sd((2, 4, part, rows), F32), sd((2, part, rows), F32),
     )
     return pl.pallas_call(
         functools.partial(grads_kernel, dims),
         out_shape=out,
         in_specs=[any_] * 14 + [vm, any_],
-        out_specs=(vm, any_, vm, any_, any_),
+        out_specs=(any_,) + (vm,) * 7,
         scratch_shapes=scratch,
         compiler_params=pltpu.CompilerParams(collective_id=1, has_side_effects=True, vmem_limit_bytes=63 * 2**20),
         name="grads",
     )(eo, ex, ao, ax, g0, g2, stem_low, joined, main_low, res_low, merge_in, tside, red_in, mside, sums, ws)
+
+
+def finish_kernel(parts, n, *refs):
+    ins, outs = refs[:n], refs[n : n + len(parts)]
+    held, sems = refs[n + len(parts) : n + 2 * len(parts)], refs[-2:]
+    steps = []
+    for k, (which, row) in enumerate(parts):
+        src, dst, by = ins[which] if row is None else ins[which].at[row], outs[k], held[k]
+        size = dst.shape[0]
+        cuts = 4 if size % 32 == 0 or size >= 2048 else 1
+        edge = [size // cuts // 8 * 8 * c for c in range(cuts)] + [size]
+        for c in range(cuts):
+            r = pl.ds(edge[c], edge[c + 1] - edge[c])
+            at = len(steps)
+            steps.append((
+                pltpu.make_async_copy(src.at[r], by.at[r], sems[0].at[at]),
+                pltpu.make_async_copy(by.at[r], dst.at[r], sems[1].at[at])))
+    for step in steps:
+        step[0].start()
+    for step in steps:
+        step[0].wait()
+        step[1].start()
+    for step in steps:
+        step[1].wait()
+
+
+def finish(arrays, parts):
+    any_ = pl.BlockSpec(memory_space=pl.ANY)
+    shapes = [arrays[which].shape if row is None else arrays[which].shape[1:] for which, row in parts]
+    return pl.pallas_call(
+        functools.partial(finish_kernel, parts, len(arrays)),
+        out_shape=tuple(jax.ShapeDtypeStruct(shape, F32) for shape in shapes),
+        in_specs=[any_] * len(arrays),
+        out_specs=(any_,) * len(parts),
+        scratch_shapes=[pltpu.VMEM(shape, F32) for shape in shapes] + [pltpu.SemaphoreType.DMA((4 * len(parts),))] * 2,
+        compiler_params=pltpu.CompilerParams(vmem_limit_bytes=63 * 2**20),
+        name="finish",
+    )(*arrays)
 
 
 def local(
@@ -872,18 +994,13 @@
     act, *kept = chain(
         dims, image_count, image_size, images[0], cotangent[0], ws, split_main, split_side,
         block_reduce, w2, block_transit, merge_weight, aff)
-    igrad, out, sums, unused, unused2 = grads(dims, *kept, ws)
+    igrad, stem, spatial, merge, transit, reduce, split, sums = grads(dims, *kept, ws)
+    act, igrad, stem, spatial, grad_merge, grad_transit, grad_reduce, grad_main, grad_side = finish(
+        [act, igrad, stem, spatial, merge, transit, reduce, split], [(k, None) for k in range(7)] + [(7, 0), (7, 1)])
     activations = act.reshape(1, grid, grid, width)
     image_grad = igrad.reshape(1, 2 * grid, 2 * grid, cin)
-    grad_stem = out[N_SPATIAL : N_SPATIAL + N_STEM].reshape(3, 3, share, width).transpose(2, 0, 1, 3)
-    spatial = out[:N_SPATIAL].reshape(N_SPATIAL, share, 4, 2, LANES).transpose(0, 3, 1, 2, 4)
-    spatial = spatial.reshape(2 * N_SPATIAL, share, half)[:9]
+    grad_stem = stem.reshape(3, 3, share, width).transpose(2, 0, 1, 3)
     grad_spatial = spatial.reshape(3, 3, share, half).transpose(2, 0, 1, 3)
-    dense = out[N_SPATIAL + N_STEM :]
-    grad_merge = dense[0:2].transpose(0, 1, 2).reshape(2 * share, width)
-    grad_transit, grad_reduce = dense[2, :, :half], dense[2, :, half:]
-    split = dense[3:5].reshape(2 * share, width)
-    grad_main, grad_side = split[:, :half], split[:, half:]
     mine = affines.shape[0] // n_dp
     whole = sums.reshape(-1, 2, LANES).transpose(0, 2, 1).reshape(-1, 2)
     affine_grad = lax.dynamic_slice_in_dim(whole, lax.axis_index("dp") * mine, mine, axis=0)

time: 292 us -> 213 us (0.73)
  Pallas kernels: 270 us -> 209 us
  local copies, waits for them, and re-layouts: 19 us -> 1.26 us
    pallas_call x1, Pallas kernels: 209 us -> 143 us  [grads(): pl.pallas_call(functools.partial(grads_kernel, dims), out_shape=out, in_s...]
    slice x5 -> x0, local copies, waits for them, and re-layouts: 8.83 us -> none  [the longest x1 3.36 us: local(): out[N_SPATIAL:N_SPATIAL + N_STEM].reshape(3, 3, share, width)]
    pallas_call x0 -> x1, Pallas kernels: none -> 7.46 us  [finish(): pl.pallas_call(functools.partial(finish_kernel, parts, len(arrays)), out_...]
    unnamed x4 -> x0, local copies, waits for them, and re-layouts: 5.1 us -> none
where the time goes in v2:
time: 213 us; the launch traced here: 212 us
  Pallas kernels  209 us (98%)
    pallas_call x1, Pallas kernels, grads(): pl.pallas_call(functools.partial(grads_kernel, dims), out_shape=out, in_s...  143 us
    pallas_call x1, Pallas kernels, chain(): pl.pallas_call(functools.partial(chain_kernel, dims), out_shape=out, in_s...  58.7 us
    pallas_call x1, Pallas kernels, finish(): pl.pallas_call(functools.partial(finish_kernel, parts, len(arrays)), out_...  7.46 us

profile of v2, /device:TPU:0, one launch (start us, length us, event | category | flops | bytes accessed | tf_op | source)
XLA Modules:
  0.0 212.3 jit_solution(1593761800512416921)
XLA Ops:
  1.9 58.7 %chain.1 = (f32[2888,128]{1,0:T(8,128)}, f32[4,256,384]{2,1,0:T(8,128)}, f32[4,256,384]{2,1,0:T(8,128)}, f32[256,384]{1,0:T(8,128)}, f32[256,384]{1,0:T(8,128)},...) custom-call(s32[1]{0:T(128)S(6)} %copy.30.count_ref, ...), custom_call_target="tpu_custom_call" | custom-call | tf_op jit(solution)/shard_map/chain/pallas_call | solution.py:428
  60.6 142.9 %grads.1 = (f32[5776,128]{1,0:T(8,128)}, f32[9,64,1024]{2,1,0:T(8,128)}, f32[9,64,512]{2,1,0:T(8,128)}, f32[128,1024]{1,0:T(8,128)}, f32[64,512]{1,0:T(8,128)}, ...) custom-call(f32[4,256,384]{2,1,0:T(8,128)} %get-tuple-element.44.eo_hbm, ...), custom_call_target="tpu_custom_call" | custom-call | tf_op jit(solution)/shard_map/grads/pallas_call | solution.py:933
  203.6 7.5 %finish.1 = (f32[2888,128]{1,0:T(8,128)}, f32[5776,128]{1,0:T(8,128)}, f32[9,64,1024]{2,1,0:T(8,128)}, f32[9,64,512]{2,1,0:T(8,128)}, f32[128,1024]{1,0:T(8,128)...) custom-call(f32[2888,128]{1,0:T(8,128)} %get-tuple-element.43.refs_0_, ...), custom_call_target="tpu_custom_call" | custom-call | tf_op jit(solution)/shard_map/finish/pallas_call | solution.py:971
  211.1 1.3 constant_dynamic-slice_fusion

commit v3 on v0

v3 whole, which is shorter than its diff:
```python
import functools

import jax
import jax.numpy as jnp
from jax import lax
from jax.experimental import pallas as pl
from jax.experimental.pallas import tpu as pltpu
from jax.sharding import PartitionSpec as P

EPS = 1e-05
F32 = jnp.float32
BF16 = jnp.bfloat16
MESH = pl.DeviceIdType.MESH
LEAD = 32
LANES = 128
TAPS = 9
UNITS = ["S%d" % k for k in range(5)] + ["T%d%d" % (k, h) for h in range(2) for k in range(5)] + ["B%d" % k for k in range(6)]
ORDERS = {}
for order, names in (
    ("1xy2", ["B0"]),
    ("xy21", ["B1", "B5"]),
    ("x1y2", ["B2"]),
    ("y12x", ["B3"]),
    ("yx21", ["B4"]),
    ("x12", ["S0", "S1", "S2"]),
    ("12x", ["S3"]),
    ("1x2", ["S4"]),
    ("yx2", ["T00", "T01", "T11", "T21", "T30", "T41"]),
    ("y2x", ["T10"]),
    ("xy2", ["T20", "T31", "T40"]),
):
    for name in names:
        ORDERS[name] = order
TOKENS = [
    "sync0", "sync1", "sync2", "sync3", "sync4", "sync5", "B0", "B2", "sync6", "B0", "B1", "sync7", "B1", "end",
    "B3", "B5", "B0", "B5", "B4", "B1", "B4", "B3", "B2", "FW", "PS", "B0", "PT", "S2", "P0", "B1", "I", "B4",
    "T10", "S1", "T00", "B3", "B0", "I", "B2", "T30", "I", "T40", "B5", "B1", "B4", "B3", "T20", "S2", "I", "P1",
    "T00", "B0", "T10", "T31", "B1", "T11", "S3", "T41", "T40", "B5", "S2", "B4", "T21", "T10", "I", "T30", "B3",
    "I", "S1", "B2", "T41", "T11", "S3", "T00", "T01", "S4", "B4", "T31", "T21", "T30", "T40", "B2", "T41", "S0",
    "B5", "T01", "S1", "B4", "S4", "S2", "T21", "S3", "T01", "T11", "B0", "T10", "T00", "S1", "T20", "B5", "T31",
    "S0", "B2", "I", "T01", "I", "B3", "T10", "T30", "T41", "T20", "S4", "S3", "B2", "S1", "T11", "I", "S0",
    "T31", "T40", "T21", "B3", "T41", "S2", "T30", "S4", "S3", "T00", "T20", "T11", "S1", "B4", "S2", "B3", "T30",
    "B1", "B2", "B5", "S0", "B0", "T10", "T40", "T40", "T31", "T21", "T41", "S4", "T01", "T11", "T20", "S0", "B5",
    "T01", "T20", "S3", "T31", "T21", "S4", "B1", "T00", "S0"
]


def mish_parts(value):
    t = jnp.exp(-jnp.abs(value))
    positive = value >= 0
    t2 = t * t
    top = jnp.where(positive, 1.0 + 2.0 * t, t2 + 2.0 * t)
    inv = 1.0 / (top + jnp.where(positive, 2.0 * t2, 2.0))
    gate = top * inv
    slope = jnp.where(positive, t2, t) * (1.0 + t) * (4.0 * inv * inv)
    return value * gate, gate + value * slope


def dot(left, right):
    return jnp.dot(left, right, preferred_element_type=F32)


def dot_t(left, right):
    return lax.dot_general(left, right, (((1,), (1,)), ((), ())), preferred_element_type=F32)


def lane_tile(j, size=LANES):
    if isinstance(j, int):
        return pl.ds(j * size, size)
    return pl.ds(pl.multiple_of(j * size, size), size)


def share_place(share, bits):
    place = 0
    for bit in bits:
        place = 2 * place + (share >> bit) % 2
    return place


def rest_bits(n_dp):
    return list(range(n_dp.bit_length() - 2, 1, -1))


def flip(index, bit):
    low = lax.rem(index // (1 << bit), 2)
    return index + (1 - 2 * low) * (1 << bit), low


class Unit:
    def __init__(self, name, dims):
        grid, cin, width, half, n_dp, n_bn = dims
        self.name, self.kind = name, name[0]
        order = ORDERS.get(name, {"S": "1x2", "T": "yx2", "B": "xy12"}[self.kind])
        self.steps = []
        for letter in order:
            self.steps += {"x": ["x"], "y": [0], "1": [1], "2": rest_bits(n_dp)}[letter]
        self.bits = [step for step in self.steps if step != "x"]
        narrow = name in ("S4", "T40", "T41", "B2", "B3")
        rows, cols = (cin if self.kind == "B" else cin // 2), (width // 4 if narrow else width // 2)
        self.start = (rows, cols)
        self.pool = self.kind + ("n" if narrow and self.kind == "B" else "")
        self.shapes = [(rows, cols)] if self.kind == "B" else []
        for step in self.steps:
            rows, cols = (rows, cols // 2) if step == "x" else (rows // 2, cols)
            self.shapes.append((rows, cols))
        self.final = (rows, cols)
        self.n_moves = len(self.shapes)
        self.n_stages = self.n_moves + 3


def plan(dims):
    units = {name: Unit(name, dims) for name in UNITS}
    shapes, finals, message = {}, {}, 0
    for unit in units.values():
        unit.at = []
        for shape in unit.shapes:
            unit.at.append((shape, shapes.get(shape, 0)))
            shapes[shape] = shapes.get(shape, 0) + 1
        unit.across = (unit.final, finals.get(unit.final, 0))
        finals[unit.final] = finals.get(unit.final, 0) + 1
        unit.message = message
        message += unit.n_moves + 5
    fills, now = {k: [] for k in range(9)}, 8
    for token in TOKENS or ["B%d" % k for k in range(6) for unused in range(2)] + ["FW", "PS", "PT", "P0", "P1"]:
        if token[:4] == "sync":
            now = int(token[4:])
        elif token == "end":
            now = 8
        else:
            fills[now].append(token)
    stage = {name: sum(fill.count(name) for fill in fills.values()) for name in UNITS}
    while any(stage[name] < units[name].n_stages for name in UNITS):
        for name in UNITS:
            if stage[name] < units[name].n_stages:
                fills[8].append(name)
                stage[name] += 1
    kinds = ("S", "T", "B", "Bn")
    seen, count, free = {}, {kind: 0 for kind in kinds}, {kind: [] for kind in kinds}
    for k in range(9):
        for token in fills[k]:
            if token in units:
                unit = units[token]
                n = seen.get(token, 0)
                seen[token] = n + 1
                if n == 0:
                    if not free[unit.pool]:
                        free[unit.pool].append(count[unit.pool])
                        count[unit.pool] += 1
                    unit.slot = free[unit.pool].pop(0)
                elif n == 1:
                    free[unit.pool].append(unit.slot)
    return units, shapes, finals, message, fills, count


def fused_kernel(
    dims,
    count_ref, size_ref, images_hbm, cot_hbm, ws_hbm, wm_hbm, wsd_hbm, wr_hbm, w2_hbm, wt_hbm, wmg_hbm, aff_ref,
    act_hbm, igrad_hbm, out_stem, out_spatial, out_merge, out_transit, out_reduce, out_split, total_ref,
    eo_hbm, ex_hbm, ec_hbm, ao_hbm, ax_hbm, ac_hbm, g2_hbm, g0_hbm,
    landed, across_land, own_g, own_g2, mask, stat, msg, heard, sums_ref, sums_in,
    wsem, ssem, rsem, local_sem, give_sem, take_sem, m_send, m_recv, keep_sem, s_send, s_recv,
):
    grid, cin, width, half, n_dp, n_bn = dims
    units, shapes, finals, n_messages, fills, pool = plan(dims)
    shape_list, final_list = list(shapes), list(finals)
    pitch = grid + 1
    rows = own_g.shape[0] - LEAD
    blocks = rows // LANES
    share = cin // n_dp
    part = cin // 2
    quarter = width // 4
    half2 = half // 2
    n_bits = n_dp.bit_length() - 1
    wide_tiles, half_tiles = width // LANES, half // LANES
    t0, t1, t2, t3 = 0, wide_tiles, wide_tiles + half_tiles, wide_tiles + 2 * half_tiles

    dp, bn = lax.axis_index("dp"), lax.axis_index("bn")
    others = [(dp, lax.rem(bn + k, n_bn)) for k in range(1, n_bn)]
    sib, core = flip(bn, 0)
    over, cross = flip(bn, 1)
    bit_of = [flip(dp, b) for b in range(n_bits)]
    sibling, across = (dp, sib), (dp, over)
    along = [(bit_of[b][0], bn) for b in range(n_bits)]
    next_sib, pair_sib = (bit_of[0][0], sib), (bit_of[1][0], sib)
    partners = others + along + [next_sib, pair_sib]

    def remote(src, dst, send, recv, target):
        return pltpu.make_async_remote_copy(
            src_ref=src, dst_ref=dst, send_sem=send, recv_sem=recv, device_id=target, device_id_type=MESH)

    def part_of(which, size):
        return pl.ds(pl.multiple_of(which * size, size), size)

    barrier = pltpu.get_barrier_semaphore()
    for target in partners:
        pl.semaphore_signal(barrier, inc=1, device_id=target, device_id_type=MESH)

    places = lax.broadcasted_iota(jnp.int32, (rows, LANES), 0)
    row = (places * 3277) >> 16 if pitch == 20 else places // pitch
    col = places - row * pitch
    size = jnp.where(count_ref[0] > 0, size_ref[0], 0)
    mask[...] = jnp.where((row < size) & (col < size), 1.0, 0.0).astype(F32)
    own_g[rows:, :] = jnp.zeros((LEAD, width), F32)

    def put_sums(sync, j, first, second, tiles):
        msg[sync, pl.ds(j, 1), :] = first
        msg[sync, pl.ds(tiles + j, 1), :] = second

    def column_sums(sync, z, j, tiles):
        zm = z * mask[...]
        put_sums(sync, j, jnp.sum(zm, axis=0, keepdims=True), jnp.sum(zm * z, axis=0, keepdims=True), tiles)

    def matmul_stats(sync, left, weight, out, cols, ready=lambda n: None):
        def body(n, _):
            ready(n)
            z = dot(left[...], weight[:, lane_tile(n, 256)])
            out[:, lane_tile(n, 256)] = z
            for h in range(2):
                column_sums(sync, z[:, h * LANES : (h + 1) * LANES], 2 * n + h, cols // LANES)
            return 0
        lax.fori_loop(0, cols // 256, body, 0)

    def greet(sync):
        return [
            remote(msg.at[sync], heard.at[sync, bn], ssem.at[sync, k], rsem.at[sync, k], target)
            for k, target in enumerate(others)]

    def send(sync):
        heard[sync, bn] = msg[sync]
        for copy in greet(sync):
            copy.start()

    def receive(sync):
        for copy in greet(sync):
            copy.wait()
        total = heard[sync, 0]
        for k in range(1, n_bn):
            total = total + heard[sync, k]
        return total

    def set_stat(slot, total, count, first_tile, tiles):
        mean = total[0:tiles] / count
        spread = total[tiles : 2 * tiles] / count - mean * mean
        stat[slot, 0, 0:tiles, :] = mean
        stat[slot, 1, 0:tiles, :] = lax.rsqrt(spread + EPS)
        for j in range(tiles):
            stat[slot, 2, j : j + 1, :] = aff_ref[2 * (first_tile + j) : 2 * (first_tile + j) + 1, :]
            stat[slot, 3, j : j + 1, :] = aff_ref[2 * (first_tile + j) + 1 : 2 * (first_tile + j) + 2, :]

    def per_tile(tiles, body):
        def step(j, _):
            body(j, lane_tile(j))
            return 0
        lax.fori_loop(0, tiles, step, 0)

    def normed(slot, z, j, cs, r):
        scaled = (z[r, cs] - stat[slot, 0, pl.ds(j, 1), :]) * stat[slot, 1, pl.ds(j, 1), :]
        return scaled, scaled * stat[slot, 2, pl.ds(j, 1), :] + stat[slot, 3, pl.ds(j, 1), :]

    def forward(slot, z, keep, tiles, put):
        def body(j, cs):
            for b in range(blocks):
                r = pl.ds(b * LANES, LANES)
                unused, before = normed(slot, z, j, cs, r)
                act, slope = mish_parts(before)
                keep[r, cs] = slope * mask[r, :]
                put(r, cs, act * mask[r, :])
        per_tile(tiles, body)

    def backward_sums(sync, slot, z, inner_ref, j, cs, upstream, tiles):
        first = jnp.zeros((1, LANES), F32)
        second = jnp.zeros((1, LANES), F32)
        for b in range(blocks):
            r = pl.ds(b * LANES, LANES)
            inner = inner_ref[r, cs] * upstream[r, cs]
            inner_ref[r, cs] = inner
            scaled = (z[r, cs] - stat[slot, 0, pl.ds(j, 1), :]) * stat[slot, 1, pl.ds(j, 1), :]
            first = first + jnp.sum(inner, axis=0, keepdims=True)
            second = second + jnp.sum(inner * scaled, axis=0, keepdims=True)
        put_sums(sync, j, first, second, tiles)

    def set_back(slot, total, count, first_tile, tiles):
        for j in range(tiles):
            sums_ref[2 * (first_tile + j) : 2 * (first_tile + j) + 1, :] = total[tiles + j : tiles + j + 1]
            sums_ref[2 * (first_tile + j) + 1 : 2 * (first_tile + j) + 2, :] = total[j : j + 1]
        stat[slot, 4, 0:tiles, :] = total[0:tiles] / count
        stat[slot, 5, 0:tiles, :] = total[tiles : 2 * tiles] / count

    def backward(slot, z, inner_ref, tiles, put):
        def body(j, cs):
            for b in range(blocks):
                r = pl.ds(b * LANES, LANES)
                inv = stat[slot, 1, pl.ds(j, 1), :]
                scaled = (z[r, cs] - stat[slot, 0, pl.ds(j, 1), :]) * inv
                pull = mask[r, :] * (stat[slot, 4, pl.ds(j, 1), :] + scaled * stat[slot, 5, pl.ds(j, 1), :])
                value = (inner_ref[r, cs] - pull) * (inv * stat[slot, 2, pl.ds(j, 1), :])
                put(r, cs, value.astype(BF16))
        per_tile(tiles, body)

    local = {}
    stage = {name: 0 for name in units}

    def landing(unit, k):
        shape, n = unit.at[k]
        return landed[shape_list.index(shape)].at[n]

    def source(unit, k):
        return local[unit.pool](unit.slot) if k == 0 else landing(unit, k - 1)

    def move_of(unit, k):
        size_r, size_c = unit.shapes[k]
        step = "c" if unit.kind == "B" and k == 0 else unit.steps[k - (unit.kind == "B")]
        if step == "c":
            return sibling, (pl.ds(0, size_r), part_of(1 - core, size_c)), (None, part_of(core, size_c))
        if step == "x":
            return across, (pl.ds(0, size_r), part_of(1 - cross, size_c)), (None, part_of(cross, size_c))
        bit = bit_of[step][1]
        return along[step], (part_of(1 - bit, size_r), pl.ds(0, size_c)), (bit, pl.ds(0, size_c))

    def move(unit, k):
        target, gone, unused = move_of(unit, k)
        m = unit.message + k
        return remote(source(unit, k).at[gone[0], gone[1]], landing(unit, k), m_send.at[m], m_recv.at[m], target)

    def add_own(unit, k):
        unused, unused2, (bit, columns) = move_of(unit, k)
        size = unit.shapes[k][0]
        src, dst = source(unit, k), landing(unit, k)
        n = min(size, 64)

        def body(i, _):
            r = pl.ds(pl.multiple_of(i * n, n), n)
            own = r if bit is None else pl.ds(pl.multiple_of(bit * size + i * n, 8), n)
            dst[r, :] = dst[r, :] + src[own, columns]
            return 0
        lax.fori_loop(0, size // n, body, 0)

    def pieces(unit, cross_at):
        k = int(unit.name[1])
        at = 2 * core + cross_at
        taps_of = range(2 * k, min(2 * k + 2, TAPS))
        if unit.kind == "T":
            col = part_of(4 * core + 2 * int(unit.name[2]) + cross_at, LANES)
            return [(out_stem.at[t, :, col], (t - 2 * k) * LANES) for t in taps_of]
        if unit.kind == "S":
            return [(out_spatial.at[t, :, part_of(at, half // 4)], (t - 2 * k) * (half // 4)) for t in taps_of]
        if k < 2:
            return [(out_merge.at[pl.ds(k * share, share), part_of(at, quarter)], 0)]
        if k < 4:
            return [((out_transit if k == 2 else out_reduce).at[:, part_of(at, half // 4)], 0)]
        return [(out_split.at[core, pl.ds((k - 4) * share, share), part_of(cross_at, half2)], 0)]

    def arrival(unit):
        shape, n = unit.across
        return across_land[final_list.index(shape)].at[n]

    def give_across(unit):
        m = unit.message + unit.n_moves
        return remote(landing(unit, unit.n_moves - 1), arrival(unit), m_send.at[m], m_recv.at[m], across)

    def spread_piece(unit, mine):
        block = landing(unit, unit.n_moves - 1) if mine else arrival(unit)
        m = unit.message + unit.n_moves + (1 if mine else 3)
        copies = []
        for n, (place, first) in enumerate(pieces(unit, cross if mine else 1 - cross)):
            src = block.at[:, pl.ds(first, place.shape[-1])]
            copies.append(pltpu.make_async_copy(src, place, keep_sem.at[m + n]))
            copies.append(remote(src, place, m_send.at[m + n], m_recv.at[m + n], sibling))
        return copies

    def advance(name, compute):
        unit = units[name]
        k = stage[name]
        stage[name] = k + 1
        if k == 0:
            compute(unit)
            move(unit, 0).start()
        elif k <= unit.n_moves:
            move(unit, k - 1).wait()
            add_own(unit, k - 1)
            if k < unit.n_moves:
                move(unit, k).start()
            else:
                give_across(unit).start()
                for copy in spread_piece(unit, True):
                    copy.start()
        elif k == unit.n_moves + 1:
            give_across(unit).wait()
            for copy in spread_piece(unit, False):
                copy.start()
        else:
            for copy in spread_piece(unit, True) + spread_piece(unit, False):
                copy.wait()

    next_bit, pair_bit = bit_of[0][1], bit_of[1][1]
    next_bits, pair_bits = [0, 1] + rest_bits(n_dp), [1, 0] + rest_bits(n_dp)

    def field_gives(src, dst, which_of, size, first, targets):
        return [
            remote(src.at[pl.ds(0, rows), part_of(which_of(which), size)], dst.at[k], give_sem.at[first + k], take_sem.at[first + k], target)
            for k, (target, which) in enumerate(targets)]
    gives2 = field_gives(own_g2, g2_hbm, lambda w: w, half2, 0, ((sibling, 1 - core), (along[0], core), (next_sib, 1 - core)))
    gives0 = [
        field_gives(own_g, g0_hbm.at[h], lambda w, h=h: 2 * w + h, quarter, 3 + 3 * h,
                    ((sibling, 1 - core), (along[1], core), (pair_sib, 1 - core)))
        for h in range(2)]

    forwards = [
        remote(ax_hbm, ac_hbm.at[1], give_sem.at[14], take_sem.at[14], sibling),
        remote(ex_hbm, ec_hbm.at[1], give_sem.at[15], take_sem.at[15], sibling)]

    def turned_block(block, k, dst, bits, parts=1):
        for piece in range(LANES // share):
            at_row = k * LANES + piece * share
            s, h = (at_row // share) // parts, (at_row // share) % parts
            at = share_place(s, bits[h]) * share
            dst(h, pl.ds(at, share), block[piece * share : (piece + 1) * share])

    def chain_phase(wms, wr, w2, wt, wmg, taps, z0, d0, stem_low, et):
        smalls = [
            pltpu.make_async_copy(src, dst, wsem.at[2 + k])
            for k, (src, dst) in enumerate(
                [(wm_hbm, wms.at[:, pl.ds(0, half)]), (wsd_hbm, wms.at[:, pl.ds(half, half)]),
                 (wr_hbm, wr), (w2_hbm, w2), (wt_hbm, wt), (wmg_hbm, wmg)])
        ]

        def first_phase(ws, images, phases, img_row):
            load_i = pltpu.make_async_copy(images_hbm, images, wsem.at[0])

            def load_w(n):
                block = lane_tile(n, 256)
                return pltpu.make_async_copy(ws_hbm.at[:, block], ws.at[:, block], wsem.at[8 + n])
            load_i.start()
            for n in range(width // 256):
                load_w(n).start()
            for p in range(4):
                phases[p, 0:LEAD, :] = jnp.zeros((LEAD, cin), F32)
                tail = LEAD + pitch * grid
                phases[p, tail:, :] = jnp.zeros((phases.shape[1] - tail, cin), F32)
            load_i.wait()
            for line in range(2 * grid):
                slot = line % 2
                value = images[line].astype(F32)
                for k in range(cin // LANES):
                    img_row[slot, k, 0 : 2 * grid, :] = value[:, k * LANES : (k + 1) * LANES]
                start = LEAD + pitch * (line // 2)
                for odd in range(2):
                    p = 2 * (line % 2) + odd
                    for k in range(cin // LANES):
                        phases[p, start : start + grid, k * LANES : (k + 1) * LANES] = img_row[slot, k, pl.ds(odd, grid, stride=2), :]
                    phases[p, start + grid : start + grid + 1, :] = jnp.zeros((1, cin), F32)
            for k in range(TAPS):
                a, b = k // 3, k % 3
                p = 2 * (a != 1) + (b != 1)
                off = LEAD - pitch * (a == 0) - (b == 0)
                taps[:, k * cin : (k + 1) * cin] = phases[p, off : off + rows, :].astype(BF16)
            for load in smalls:
                load.start()
            matmul_stats(0, taps, ws, z0, width, lambda n: load_w(n).wait())
            msg[0, 2 * wide_tiles : 2 * wide_tiles + 8, :] = jnp.zeros((8, LANES), F32) + jnp.sum(mask[...], axis=0, keepdims=True)
            pl.semaphore_wait(barrier, len(partners))
            send(0)

            def turn_phase(p, _):
                for k in range(cin // LANES):
                    block = phases[p, LEAD : LEAD + rows, k * LANES : (k + 1) * LANES].T

                    def put(h, r, value):
                        et[p, r, :] = value
                    turned_block(block, k, put, [pair_bits])
                return 0
            lax.fori_loop(0, 4, turn_phase, 0)

        pl.run_scoped(
            first_phase, pltpu.VMEM((TAPS * cin, width), BF16), pltpu.VMEM((2 * grid, 2 * grid, cin), BF16),
            pltpu.VMEM((4, LEAD + rows, cin), F32), pltpu.VMEM((2, cin // LANES, -(-2 * grid // 8) * 8, LANES), F32))
        keep_e = pltpu.make_async_copy(et.at[0:4, part_of(pair_bit, part), :], eo_hbm, local_sem.at[0])
        give_e = remote(et.at[0:4, part_of(1 - pair_bit, part), :], ex_hbm, give_sem.at[9], take_sem.at[9], along[1])
        keep_e.start()
        give_e.start()
        own_e = [
            remote(et.at[pl.ds(2 * h, 2), part_of(pair_bit, part), :], ec_hbm.at[0, pl.ds(2 * h, 2)],
                   give_sem.at[11 + h], take_sem.at[11 + h], sibling)
            for h in range(2)]

        def rest_phase(
            z1, d1, z2, d2, wide, narrow, main_path, apad, gpad, back, joined, main_low, res_low, mside, turned, act, cot_in, tile,
        ):
            z3 = own_g.at[pl.ds(0, rows)]
            i3, cot = wide.at[0, pl.ds(0, rows)], wide.at[1, pl.ds(0, rows)]
            merge_in, tside, red_in = stem_low, joined, main_low
            local["B"] = lambda slot: wide.at[slot]
            local["Bn"] = lambda slot: narrow.at[slot]
            load_cot = pltpu.make_async_copy(cot_hbm, cot_in, local_sem.at[1])
            load_cot.start()
            for ref in (apad, gpad):
                ref[0:LEAD, :] = jnp.zeros((LEAD, half), F32)
                ref[LEAD + rows :, :] = jnp.zeros((LEAD, half), F32)

            def turn(src, first, parts):
                for k in range(parts * half // LANES):
                    block = src[:, k * LANES : (k + 1) * LANES].astype(F32).T

                    def put(h, r, value):
                        turned[first + h, r, :] = value.astype(BF16)
                    turned_block(block, k, put, [units["B%d" % (first + h)].bits for h in range(parts)], parts)

            def compute(unit):
                k = int(unit.name[1])
                right = [merge_in, merge_in, tside, red_in, mside, mside][k]
                dst = local[unit.pool](unit.slot)
                for n in range(2 * unit.start[1] // 256):
                    dst[:, pl.ds(n * 256, 256)] = dot(turned[k], right[:, pl.ds(n * 256, 256)])

            def fill(sync):
                for token in fills[sync]:
                    advance(token, compute)

            total = receive(0)
            count = total[2 * wide_tiles : 2 * wide_tiles + 1, 0:1]
            set_stat(0, total, count, t0, wide_tiles)

            def put_stem(r, cs, value):
                stem_low[r, cs] = value.astype(BF16)
            forward(0, z0, d0, wide_tiles, put_stem)
            smalls[0].wait()
            smalls[1].wait()
            for n in range(half // 256):
                y = dot(stem_low[...], wms[:, lane_tile(n, 256)])
                main_path[:, lane_tile(n, 256)] = y
                main_low[:, lane_tile(n, 256)] = y.astype(BF16)
            smalls[2].wait()
            matmul_stats(1, main_low, wr, z1, half)
            send(1)
            own_e[0].start()
            for n in range(half // 256):
                y = dot(stem_low[...], wms[:, lane_tile(half // 256 + n, 256)])
                joined[:, lane_tile(half // 256 + n, 256)] = y.astype(BF16)
            turn(stem_low, 4, 2)
            set_stat(1, receive(1), count, t1, half_tiles)

            def put_reduce(r, cs, value):
                apad[pl.ds(LEAD + r.start, r.size), cs] = value.astype(BF16).astype(F32)
            forward(1, z1, d1, half_tiles, put_reduce)
            for k in range(TAPS):
                off = LEAD + pitch * (k // 3 - 1) + k % 3 - 1
                taps[:, k * half : (k + 1) * half] = apad[off : off + rows, :].astype(BF16)
            smalls[3].wait()
            matmul_stats(2, taps, w2, z2, half)
            send(2)
            own_e[1].start()
            for k in range(half // LANES):
                def put_a(h, r, value):
                    et[4, r, :] = value
                turned_block(apad[LEAD : LEAD + rows, k * LANES : (k + 1) * LANES].T, k, put_a, [next_bits])
            keep_a = pltpu.make_async_copy(et.at[4, part_of(next_bit, part), :], ao_hbm, local_sem.at[2])
            give_a = remote(et.at[4, part_of(1 - next_bit, part), :], ax_hbm, give_sem.at[10], take_sem.at[10], along[0])
            own_a = remote(et.at[4, part_of(next_bit, part), :], ac_hbm.at[0], give_sem.at[13], take_sem.at[13], sibling)
            keep_a.start()
            give_a.start()
            turn(main_low, 3, 1)
            load_cot.wait()
            for r in range(grid):
                cot[r * pitch : r * pitch + grid, :] = cot_in[r].astype(F32)
                cot[r * pitch + grid : (r + 1) * pitch, :] = jnp.zeros((1, width), F32)
            cot[grid * pitch :, :] = jnp.zeros((rows - grid * pitch, width), F32)
            set_stat(2, receive(2), count, t2, half_tiles)

            def put_spatial(r, cs, value):
                res_low[r, cs] = (main_path[r, cs] + value).astype(BF16)
            forward(2, z2, d2, half_tiles, put_spatial)
            smalls[4].wait()
            for n in range(half // 256):
                joined[:, lane_tile(n, 256)] = dot(res_low[...], wt[:, lane_tile(n, 256)]).astype(BF16)
            smalls[5].wait()
            matmul_stats(3, joined, wmg, z3, width)
            send(3)
            own_a.start()
            turn(joined, 0, 2)
            set_stat(3, receive(3), count, t3, wide_tiles)

            def merge_tile(j, cs):
                for b in range(blocks):
                    r = pl.ds(b * LANES, LANES)
                    unused, before = normed(3, z3, j, cs, r)
                    value, slope = mish_parts(before)
                    tile[r, :] = value * mask[r, :]
                    i3[r, cs] = slope * mask[r, :]
                backward_sums(4, 3, z3, i3, j, cs, cot, wide_tiles)
                cot[:, cs] = tile[...]
            per_tile(wide_tiles, merge_tile)
            send(4)

            def act_tile(j, cs):
                for line in range(grid):
                    act[pl.ds(line * grid * wide_tiles + j, grid, stride=wide_tiles), :] = cot[line * pitch : line * pitch + grid, cs]
            per_tile(wide_tiles, act_tile)
            store_act = pltpu.make_async_copy(act, act_hbm, local_sem.at[3])
            store_act.start()
            turn(res_low, 2, 1)
            fill(4)
            set_back(3, receive(4), count, t3, wide_tiles)

            def put_merge(r, cs, value):
                merge_in[r, cs] = value
            backward(3, z3, i3, wide_tiles, put_merge)
            for n in range(width // 256):
                tside[:, lane_tile(n, 256)] = dot_t(merge_in[...], wmg[lane_tile(n, 256), :]).astype(BF16)
            for n in range(half // 256):
                back[:, lane_tile(n, 256)] = dot_t(tside[:, 0:half], wt[lane_tile(n, 256), :])

            def spatial_tile(j, cs):
                backward_sums(5, 2, z2, d2, j, cs, back, half_tiles)
            per_tile(half_tiles, spatial_tile)
            send(5)
            fill(5)
            set_back(2, receive(5), count, t2, half_tiles)

            def put_spatial_in(r, cs, value):
                gpad[pl.ds(LEAD + r.start, r.size), cs] = value.astype(F32)
                own_g2[r, cs] = value.astype(F32)
            backward(2, z2, d2, half_tiles, put_spatial_in)
            for give in gives2:
                give.start()
            for k in range(TAPS):
                off = LEAD - pitch * (k // 3 - 1) - (k % 3 - 1)
                taps[:, k * half : (k + 1) * half] = gpad[off : off + rows, :].astype(BF16)

            def reduce_columns(n, _):
                value = jnp.zeros((rows, 256), F32)
                for k in range(TAPS):
                    value = value + dot_t(taps[:, k * half : (k + 1) * half], w2[pl.ds(pl.multiple_of(k * half + n * 256, 256), 256), :])
                main_path[:, lane_tile(n, 256)] = value
                return 0
            lax.fori_loop(0, half // 256, reduce_columns, 0)

            def reduce_tile(j, cs):
                backward_sums(6, 1, z1, d1, j, cs, main_path, half_tiles)
            per_tile(half_tiles, reduce_tile)
            send(6)
            mside[:, half : 2 * half] = tside[:, half : 2 * half]
            fill(6)
            set_back(1, receive(6), count, t1, half_tiles)

            def put_reduce_in(r, cs, value):
                red_in[r, cs] = value
            backward(1, z1, d1, half_tiles, put_reduce_in)
            for n in range(half // 256):
                mside[:, lane_tile(n, 256)] = (back[:, lane_tile(n, 256)] + dot_t(red_in[...], wr[lane_tile(n, 256), :])).astype(BF16)

            def stem_columns(n, _):
                z3[:, lane_tile(n, 256)] = dot_t(mside[...], wms[lane_tile(n, 256), :])
                return 0
            lax.fori_loop(0, width // 256, stem_columns, 0)

            def stem_tile(j, cs):
                backward_sums(7, 0, z0, d0, j, cs, z3, wide_tiles)
            per_tile(wide_tiles, stem_tile)
            send(7)
            fill(7)
            set_back(0, receive(7), count, t0, wide_tiles)

            def put_stem_in(r, cs, value):
                own_g[r, cs] = value.astype(F32)
            backward(0, z0, d0, wide_tiles, put_stem_in)
            for gives in gives0:
                for give in gives:
                    give.start()
            while any(units[name].kind == "B" and stage[name] < 2 for name in units) or "FW" in fills[8]:
                token = fills[8].pop(0)
                if token == "FW":
                    give_e.wait()
                    give_a.wait()
                    for forward_copy in forwards:
                        forward_copy.start()
                else:
                    advance(token, compute)
            for copy in own_e + [own_a, keep_e, keep_a, store_act]:
                copy.wait()

        pl.run_scoped(
            rest_phase,
            pltpu.VMEM((rows, half), F32), pltpu.VMEM((rows, half), F32), pltpu.VMEM((rows, half), F32), pltpu.VMEM((rows, half), F32),
            pltpu.VMEM((max(2, pool["B"]), cin, width), F32), pltpu.VMEM((pool["Bn"], cin, half), F32),
            pltpu.VMEM((rows, half), F32), pltpu.VMEM((LEAD + rows + LEAD, half), F32), pltpu.VMEM((LEAD + rows + LEAD, half), F32),
            pltpu.VMEM((rows, half), F32), pltpu.VMEM((rows, 2 * half), BF16), pltpu.VMEM((rows, half), BF16),
            pltpu.VMEM((rows, half), BF16), pltpu.VMEM((rows, 2 * half), BF16), pltpu.VMEM((6, cin, rows), BF16),
            pltpu.VMEM((grid * grid * wide_tiles, LANES), F32), pltpu.VMEM((grid, grid, width), BF16), pltpu.VMEM((rows, LANES), F32))

    pl.run_scoped(
        chain_phase,
        pltpu.VMEM((width, 2 * half), BF16), pltpu.VMEM((half, half), BF16), pltpu.VMEM((TAPS * half, half), BF16),
        pltpu.VMEM((half, half), BF16), pltpu.VMEM((width, width), BF16), pltpu.VMEM((rows, TAPS * cin), BF16),
        pltpu.VMEM((rows, width), F32), pltpu.VMEM((rows, width), F32), pltpu.VMEM((rows, width), BF16),
        pltpu.VMEM((5, cin, rows), F32))

    def last_phase(g2r, g0r, at_land, at_cat, spatial, et_land, et_cat, shifted, own_shift, image, weight, stem_blocks, igrad):
        local["S"] = lambda slot: spatial.at[slot]
        local["T"] = lambda slot: stem_blocks.at[slot]
        offsets = (0, 1, pitch, pitch + 1)
        image_taps = [4, 3, 5, 1, 7, 0, 2, 6, 8]
        done = []
        sums_done = []

        def load_weight(n):
            k = image_taps[n]
            return pltpu.make_async_copy(ws_hbm.at[pl.ds(k * cin, cin)], weight.at[n % 2], wsem.at[n % 2])
        load_weight(0).start()
        own_parts = [
            pltpu.make_async_copy(src, dst, local_sem.at[9 + k])
            for k, (src, dst) in enumerate(
                ((ao_hbm, at_land.at[0]), (ax_hbm, at_land.at[1]), (eo_hbm, et_land.at[0]), (ex_hbm, et_land.at[1])))]
        for load in own_parts:
            load.start()

        def sums_step(k):
            return remote(total_ref if k else sums_ref, sums_in.at[k], s_send.at[k], s_recv.at[k], along[k])

        def sums_next():
            k = len(sums_done)
            if k < n_bits:
                sums_done.append(k)
                sums_step(k).wait()
                total_ref[...] = (total_ref[...] if k else sums_ref[...]) + sums_in[k]
                if k + 1 < n_bits:
                    sums_step(k + 1).start()
        sums_step(0).start()
        for k in range(4):
            g2r[k, 0:LEAD, :] = jnp.zeros((LEAD, half2), F32)
            g2r[k, LEAD + rows :, :] = jnp.zeros((LEAD, half2), F32)
            for h in range(2):
                g0r[h, k, rows:, :] = jnp.zeros((LEAD, quarter), F32)

        def tap(k):
            a, b = k // 3, k % 3
            return 2 * (a != 1) + (b != 1), 2 * (a == 0) + (b == 0)

        def fetch(pairs, first):
            loads = [pltpu.make_async_copy(src, dst, local_sem.at[first + k]) for k, (src, dst) in enumerate(pairs)]
            for load in loads:
                load.start()
            for load in loads:
                load.wait()

        def compute(unit):
            k = int(unit.name[1])
            c = unit.start[1] // 2
            dst = local[unit.pool](unit.slot)
            for h in range(2):
                t = 2 * k + h
                if t == TAPS:
                    continue
                if unit.kind == "T":
                    p, sh = tap(t)
                    value = dot(et_cat[p], shifted[int(unit.name[2]), sh])
                else:
                    off = LEAD - pitch * (t // 3 - 1) - (t % 3 - 1)
                    right = jnp.concatenate([g2r[s, off : off + rows, :].astype(BF16) for s in range(4)], axis=0)
                    value = dot(at_cat[...], right)
                for x in range(2):
                    dst[:, c * x + LANES * h : c * x + LANES * (h + 1)] = value[:, LANES * x : LANES * (x + 1)]

        def image_step():
            n = len(done)
            k = image_taps[n]
            p, sh = tap(k)
            if n + 1 < TAPS:
                load_weight(n + 1).start()
            load_weight(n).wait()
            for m in range(cin // 256):
                c = slice(m * 256, (m + 1) * 256)
                value = dot_t(own_shift[sh], weight[n % 2, c, :])
                image[:, c] = value if k in (4, 3, 1, 0) else image[:, c] + value
            done.append(k)
            if k in (4, 5, 7, 8):
                for r in range(grid):
                    for m in range(cin // LANES):
                        start = ((2 * r + p // 2) * 2 * grid + p % 2) * (cin // LANES) + m
                        igrad[pl.ds(start, grid, stride=2 * cin // LANES), :] = image[r * pitch : r * pitch + grid, m * LANES : (m + 1) * LANES]
            if len(done) == TAPS:
                pltpu.make_async_copy(igrad, igrad_hbm, local_sem.at[8]).start()

        for token in fills[8]:
            if token == "PS":
                forwards[0].wait()
                own_parts[0].wait()
                own_parts[1].wait()
                for give in gives2:
                    give.wait()
                fetch([(ac_hbm.at[0], at_land.at[2]), (ac_hbm.at[1], at_land.at[3])]
                      + [(g2_hbm.at[s], g2r.at[s + 1, pl.ds(LEAD, rows)]) for s in range(3)]
                      + [(own_g2.at[:, part_of(core, half2)], g2r.at[0, pl.ds(LEAD, rows)])], 0)
                for slot, n in enumerate((0, 2, 1, 3)):
                    at_cat[:, slot * rows : (slot + 1) * rows] = at_land[n].astype(BF16)
                sums_next()
            elif token == "PT":
                forwards[1].wait()
                own_parts[2].wait()
                own_parts[3].wait()
                fetch([(ec_hbm.at[0], et_land.at[2]), (ec_hbm.at[1], et_land.at[3])], 0)
                for p in range(4):
                    for slot, n in enumerate((0, 2, 1, 3)):
                        et_cat[p, :, slot * rows : (slot + 1) * rows] = et_land[n, p].astype(BF16)
                for sh, off in enumerate(offsets):
                    own_shift[sh] = own_g[off : off + rows, :].astype(BF16)
                sums_next()
            elif token in ("P0", "P1"):
                h = int(token[1])
                for give in gives0[h]:
                    give.wait()
                fetch([(g0_hbm.at[h, s], g0r.at[h, s + 1, pl.ds(0, rows)]) for s in range(3)]
                      + [(own_g.at[pl.ds(0, rows), part_of(2 * core + h, quarter)], g0r.at[h, 0, pl.ds(0, rows)])], 0)
                for sh, off in enumerate(offsets):
                    for s in range(4):
                        shifted[h, sh, s * rows : (s + 1) * rows, :] = g0r[h, s, off : off + rows, :].astype(BF16)
                sums_next()
            elif token == "I":
                if len(done) < TAPS:
                    image_step()
            elif token in units:
                advance(token, compute)
        while len(done) < TAPS:
            image_step()
        for k in range(n_bits):
            sums_next()
        pltpu.make_async_copy(igrad, igrad_hbm, local_sem.at[8]).wait()

    pl.run_scoped(
        last_phase,
        pltpu.VMEM((4, LEAD + rows + LEAD, half2), F32), pltpu.VMEM((2, 4, rows + LEAD, quarter), F32),
        pltpu.VMEM((4, part, rows), F32), pltpu.VMEM((part, 4 * rows), BF16), pltpu.VMEM((pool["S"], part, width // 2), F32),
        pltpu.VMEM((4, 4, part, rows), F32), pltpu.VMEM((4, part, 4 * rows), BF16),
        pltpu.VMEM((2, 4, 4 * rows, quarter), BF16), pltpu.VMEM((4, rows, width), BF16), pltpu.VMEM((rows, cin), F32),
        pltpu.VMEM((2, cin, width), BF16), pltpu.VMEM((pool["T"], part, width // 2), F32),
        pltpu.VMEM((4 * grid * grid * (cin // LANES), LANES), F32))


def fused(dims, count, size, images, cot, ws, wm, wsd, wr, w2, wt, wmg, aff):
    grid, cin, width, half, n_dp, n_bn = dims
    units, shapes, finals, n_messages, fills, pool = plan(dims)
    rows = -(-grid * (grid + 1) // LANES) * LANES
    share, part = cin // n_dp, cin // 2
    tiles = width // LANES
    n_bits = n_dp.bit_length() - 1
    sd, dma = jax.ShapeDtypeStruct, pltpu.SemaphoreType.DMA
    vm, any_, sm = (pl.BlockSpec(memory_space=space) for space in (pltpu.VMEM, pl.ANY, pltpu.SMEM))
    out = (
        sd((grid * grid * tiles, LANES), F32), sd((4 * grid * grid * (cin // LANES), LANES), F32),
        sd((TAPS, share, width), F32), sd((TAPS, share, half), F32), sd((2 * share, width), F32),
        sd((share, half), F32), sd((share, half), F32), sd((2, 2 * share, half), F32), sd(aff.shape, F32),
        sd((4, part, rows), F32), sd((4, part, rows), F32), sd((2, 4, part, rows), F32),
        sd((part, rows), F32), sd((part, rows), F32), sd((2, part, rows), F32),
        sd((3, rows, half // 2), F32), sd((2, 3, rows, width // 4), F32),
    )
    scratch = [
        [pltpu.VMEM((n,) + shape, F32) for shape, n in shapes.items()],
        [pltpu.VMEM((n,) + shape, F32) for shape, n in finals.items()],
        pltpu.VMEM((rows + LEAD, width), F32), pltpu.VMEM((rows, half), F32),
        pltpu.VMEM((rows, LANES), F32), pltpu.VMEM((4, 6, 8, LANES), F32),
        pltpu.VMEM((8, 3 * tiles, LANES), F32), pltpu.VMEM((8, n_bn, 3 * tiles, LANES), F32),
        pltpu.VMEM(aff.shape, F32), pltpu.VMEM((n_bits,) + aff.shape, F32),
        dma((8 + width // 256,)), dma((8, n_bn - 1)), dma((8, n_bn - 1)), dma((16,)), dma((16,)), dma((16,)),
        dma((n_messages,)), dma((n_messages,)), dma((n_messages,)), dma((n_bits,)), dma((n_bits,)),
    ]
    return pl.pallas_call(
        functools.partial(fused_kernel, dims),
        out_shape=out,
        in_specs=[sm, sm] + [any_] * 9 + [vm],
        out_specs=(any_,) * 8 + (vm,) + (any_,) * 8,
        scratch_shapes=scratch,
        compiler_params=pltpu.CompilerParams(collective_id=0, has_side_effects=True, vmem_limit_bytes=64 * 2**20 - 65536),
        name="section",
    )(count, size, images, cot, ws, wm, wsd, wr, w2, wt, wmg, aff)


def finish_kernel(parts, n, tiles, sums_hbm, *refs):
    ins, outs, affine_hbm = refs[:n], refs[n : n + len(parts)], refs[n + len(parts)]
    held, (sums, affine, sem_a), sems = refs[n + len(parts) + 1 : n + 2 * len(parts) + 1], refs[-5:-2], refs[-2:]
    load_sums = pltpu.make_async_copy(sums_hbm, sums, sem_a.at[0])
    store_affine = pltpu.make_async_copy(affine, affine_hbm, sem_a.at[1])
    load_sums.start()
    steps = []
    for k, (which, row) in enumerate(parts):
        src, dst, by = ins[which] if row is None else ins[which].at[row], outs[k], held[k]
        size = dst.shape[0]
        cuts = 4 if size % 32 == 0 or size >= 2048 else 1
        edge = [size // cuts // 8 * 8 * c for c in range(cuts)] + [size]
        for c in range(cuts):
            r = pl.ds(edge[c], edge[c + 1] - edge[c])
            at = len(steps)
            steps.append((
                pltpu.make_async_copy(src.at[r], by.at[r], sems[0].at[at]),
                pltpu.make_async_copy(by.at[r], dst.at[r], sems[1].at[at])))
    for step in steps:
        step[0].start()
    load_sums.wait()
    first = 2 * tiles * lax.axis_index("dp")
    for t in range(affine.shape[0]):
        for c in range(2):
            affine[t, c : c + 1, :] = sums[pl.ds(first + 2 * t + c, 1), :]
    store_affine.start()
    for step in steps:
        step[0].wait()
        step[1].start()
    for step in steps:
        step[1].wait()
    store_affine.wait()


def finish(sums, tiles, arrays, parts):
    any_ = pl.BlockSpec(memory_space=pl.ANY)
    affine = (max(1, tiles), 2, LANES)
    shapes = [arrays[which].shape if row is None else arrays[which].shape[1:] for which, row in parts]
    return pl.pallas_call(
        functools.partial(finish_kernel, parts, len(arrays), tiles),
        out_shape=tuple(jax.ShapeDtypeStruct(shape, F32) for shape in shapes + [affine]),
        in_specs=[any_] * (len(arrays) + 1),
        out_specs=(any_,) * (len(parts) + 1),
        scratch_shapes=[pltpu.VMEM(shape, F32) for shape in shapes + [sums.shape, affine]] + [pltpu.SemaphoreType.DMA((2,))] + [pltpu.SemaphoreType.DMA((4 * len(parts),))] * 2,
        compiler_params=pltpu.CompilerParams(vmem_limit_bytes=63 * 2**20),
        name="finish",
    )(sums, *arrays)


def local(
    images, image_count, image_size, cotangent, stem_weight, split_main, split_side,
    block_reduce, block_spatial, block_transit, merge_weight, affines,
):
    n_dp, n_bn = lax.axis_size("dp"), lax.axis_size("bn")
    grid, cin = cotangent.shape[1], images.shape[3]
    width, half = merge_weight.shape[0], split_main.shape[1]
    share = cin // n_dp
    dims = (grid, cin, width, half, n_dp, n_bn)
    ws = stem_weight.transpose(1, 2, 0, 3).reshape(9 * cin, width)
    w2 = block_spatial.transpose(1, 2, 0, 3).reshape(9 * half, half)
    aff = affines.reshape(-1, LANES, 2).transpose(0, 2, 1).reshape(-1, LANES)
    act, igrad, stem, spatial, merge, transit, reduce, split, sums, *unused = fused(
        dims, image_count, image_size, images[0], cotangent[0], ws, split_main, split_side,
        block_reduce, w2, block_transit, merge_weight, aff)
    mine = affines.shape[0] // n_dp
    act, igrad, stem, spatial, grad_merge, grad_transit, grad_reduce, grad_main, grad_side, affine = finish(
        sums, mine // LANES, [act, igrad, stem, spatial, merge, transit, reduce, split], [(k, None) for k in range(7)] + [(7, 0), (7, 1)])
    activations = act.reshape(1, grid, grid, width)
    image_grad = igrad.reshape(1, 2 * grid, 2 * grid, cin)
    grad_stem = stem.reshape(3, 3, share, width).transpose(2, 0, 1, 3)
    grad_spatial = spatial.reshape(3, 3, share, half).transpose(2, 0, 1, 3)
    if mine % LANES == 0:
        affine_grad = affine.transpose(0, 2, 1).reshape(mine, 2)
    else:
        whole = sums.reshape(-1, 2, LANES).transpose(0, 2, 1).reshape(-1, 2)
        affine_grad = lax.dynamic_slice_in_dim(whole, lax.axis_index("dp") * mine, mine, axis=0)
    return (activations, image_grad, grad_stem, grad_main, grad_side, grad_reduce, grad_spatial, grad_transit, grad_merge, affine_grad)


def solution(mesh):
    rows = P(("dp", "bn"), None, None, None)
    return jax.shard_map(
        local,
        mesh=mesh,
        in_specs=(rows, P(("dp", "bn")), P(("dp", "bn")), rows) + (P(),) * 8,
        out_specs=(
            rows, rows, P("dp", None, None, None), P("dp", None), P("dp", None), P("dp", None),
            P("dp", None, None, None), P("dp", None), P("dp", None), P("dp", None),
        ),
        check_vma=False,
    )
```

time: 1170 us -> 195 us (0.17); the launches traced: 1160 us -> 195 us
  waiting for transfers between devices: 569 us -> 0 us
  local copies, waits for them, and re-layouts: 344 us -> 0 us
  Pallas kernels: 0 us -> 193 us
  matrix products: 123 us -> 0 us
  other arithmetic: 53.4 us -> 0 us
  blocking collectives: 52.1 us -> 0 us
  between operations: 16.7 us -> 2.11 us
    unnamed x3 -> x0, waiting for transfers between devices: 569 us -> none
    pallas_call x0 -> x2, Pallas kernels: none -> 193 us  [the longest x1 185 us: fused(): pl.pallas_call(functools.partial(fused_kernel, dims), out_shape=out, in_s...]
    dot_general x72 -> x0, matrix products: 123 us -> none  [the longest x24 51.6 us: matmul(): return jnp.dot(left, right, preferred_element_type=jnp.float32)]
    slice x22 -> x0, local copies, waits for them, and re-layouts: 91.7 us -> none  [the longest x9 51.6 us: stride_taps(): padded[:, a:a + reach:2, b:b + reach:2, :].reshape(-1, field.shape[3])]
    another operation x7 -> x0, local copies, waits for them, and re-layouts: 91.4 us -> none  [the longest x2 54.1 us: taps_grad(): stacked = jnp.stack([outer_sum(tap, upstream) for tap in taps], axis=1)]
    unnamed x161 -> x0, local copies, waits for them, and re-layouts: 73 us -> none
    reshape x35 -> x0, local copies, waits for them, and re-layouts: 59.7 us -> none  [the longest x6 17 us: reduce_grads(): flat = jnp.concatenate([g.reshape(wide * group, -1) for g in grads], axis=1)]
    psum x8 -> x0, blocking collectives: 52.1 us -> none  [the longest x4 26.7 us: normalize(): total, square, count = lax.psum((total, square, local_count), 'bn')]
  transfers between devices with their start and end apart: 2 -> 0, of which waited for: 1 -> 0; matrix products, arithmetic and copies ran while one was open for 10% -> 0% of each run, Pallas kernels for 0% -> 0%
where the time goes in v3:
time: 195 us
  Pallas kernels  193 us (99%)
  between operations  2.11 us (1%)
    pallas_call x1, Pallas kernels, fused(): pl.pallas_call(functools.partial(fused_kernel, dims), out_shape=out, in_s...  185 us
    pallas_call x1, Pallas kernels, finish(): pl.pallas_call(functools.partial(finish_kernel, parts, len(arrays), tiles...  7.62 us

profile of v3, /device:TPU:0, one launch (start us, length us, event | category | flops | bytes accessed | tf_op | source)
XLA Modules:
  0.0 194.8 jit_solution(17638869445445177290)
XLA Ops:
  1.9 185.1 %section.1 = (f32[2888,128]{1,0:T(8,128)}, f32[5776,128]{1,0:T(8,128)}, f32[9,64,1024]{2,1,0:T(8,128)}, f32[9,64,512]{2,1,0:T(8,128)}, f32[128,1024]{1,0:T(8,128...) custom-call(s32[1]{0:T(128)S(6)} %copy.28.count_ref, ...), custom_call_target="tpu_custom_call" | custom-call | tf_op jit(solution)/shard_map/section/pallas_call | solution.py:865
  187.0 7.6 %finish.1 = (f32[2888,128]{1,0:T(8,128)}, f32[5776,128]{1,0:T(8,128)}, f32[9,64,1024]{2,1,0:T(8,128)}, f32[9,64,512]{2,1,0:T(8,128)}, f32[128,1024]{1,0:T(8,128)...) custom-call(f32[48,128]{1,0:T(8,128)} %get-tuple-element.29.sums_hbm, ...), custom_call_target="tpu_custom_call" | custom-call | tf_op jit(solution)/shard_map/finish/pallas_call | solution.py:914

commit v4 on v3

--- a/solution.py
+++ b/solution.py
@@ -22,26 +22,26 @@
     ("x1y2", ["B2"]),
     ("y12x", ["B3"]),
     ("yx21", ["B4"]),
-    ("x12", ["S0", "S1", "S2"]),
-    ("12x", ["S3"]),
+    ("x12", ["S0", "S1", "S3"]),
+    ("12x", ["S2"]),
     ("1x2", ["S4"]),
-    ("yx2", ["T00", "T01", "T11", "T21", "T30", "T41"]),
+    ("yx2", ["T00", "T11", "T21", "T30", "T31", "T41"]),
+    ("xy2", ["T01", "T20", "T40"]),
     ("y2x", ["T10"]),
-    ("xy2", ["T20", "T31", "T40"]),
 ):
     for name in names:
         ORDERS[name] = order
 TOKENS = [
-    "sync0", "sync1", "sync2", "sync3", "sync4", "sync5", "B0", "B2", "sync6", "B0", "B1", "sync7", "B1", "end",
-    "B3", "B5", "B0", "B5", "B4", "B1", "B4", "B3", "B2", "FW", "PS", "B0", "PT", "S2", "P0", "B1", "I", "B4",
-    "T10", "S1", "T00", "B3", "B0", "I", "B2", "T30", "I", "T40", "B5", "B1", "B4", "B3", "T20", "S2", "I", "P1",
-    "T00", "B0", "T10", "T31", "B1", "T11", "S3", "T41", "T40", "B5", "S2", "B4", "T21", "T10", "I", "T30", "B3",
-    "I", "S1", "B2", "T41", "T11", "S3", "T00", "T01", "S4", "B4", "T31", "T21", "T30", "T40", "B2", "T41", "S0",
-    "B5", "T01", "S1", "B4", "S4", "S2", "T21", "S3", "T01", "T11", "B0", "T10", "T00", "S1", "T20", "B5", "T31",
-    "S0", "B2", "I", "T01", "I", "B3", "T10", "T30", "T41", "T20", "S4", "S3", "B2", "S1", "T11", "I", "S0",
-    "T31", "T40", "T21", "B3", "T41", "S2", "T30", "S4", "S3", "T00", "T20", "T11", "S1", "B4", "S2", "B3", "T30",
-    "B1", "B2", "B5", "S0", "B0", "T10", "T40", "T40", "T31", "T21", "T41", "S4", "T01", "T11", "T20", "S0", "B5",
-    "T01", "T20", "S3", "T31", "T21", "S4", "B1", "T00", "S0"
+    "sync0", "sync1", "sync2", "sync3", "sync4", "sync5", "B0", "sync6", "B0", "B1", "sync7", "B1", "end", "B2",
+    "B3", "B5", "B0", "B5", "B4", "B1", "B4", "B3", "B2", "FW", "PS", "B0", "S3", "PT", "I", "P0", "T10", "B4",
+    "T40", "B1", "I", "T00", "B3", "S1", "B0", "T30", "B2", "I", "I", "B5", "I", "B1", "B4", "B3", "I", "S3",
+    "T20", "P1", "T00", "T10", "T01", "B0", "T11", "T41", "S2", "B3", "B5", "S3", "T10", "T40", "T21", "B4", "I",
+    "T30", "B1", "B2", "S1", "T41", "T00", "T11", "S2", "T31", "S4", "B4", "T01", "T21", "T30", "B2", "B3", "T41",
+    "S0", "B5", "T31", "T11", "B3", "T40", "S2", "S4", "T20", "S1", "T21", "S3", "T31", "T41", "B2", "B0", "T11",
+    "T00", "B5", "S1", "S0", "T01", "S4", "S2", "T31", "T10", "B1", "B4", "T20", "T30", "T00", "I", "S1", "T21",
+    "T01", "S0", "I", "T11", "T40", "B0", "S3", "B5", "S4", "T10", "T20", "S0", "S2", "B3", "T01", "B2", "T41",
+    "T40", "T01", "T21", "S2", "T30", "T20", "T31", "S4", "S0", "S3", "T11", "T40", "T20", "B4", "T31", "T30",
+    "T21", "T10", "T41", "S0", "T00", "S4", "B2", "B1", "S1", "B5"
 ]
 
 
@@ -202,6 +202,8 @@
     mask[...] = jnp.where((row < size) & (col < size), 1.0, 0.0).astype(F32)
     own_g[rows:, :] = jnp.zeros((LEAD, width), F32)
 
+    norms = ((0, t0, wide_tiles), (1, t1, half_tiles), (2, t2, half_tiles), (3, t3, wide_tiles))
+
     def put_sums(sync, j, first, second, tiles):
         msg[sync, pl.ds(j, 1), :] = first
         msg[sync, pl.ds(tiles + j, 1), :] = second
@@ -220,22 +222,25 @@
             return 0
         lax.fori_loop(0, cols // 256, body, 0)
 
+    lines = [pl.ds(0, n) for n in (
+        2 * wide_tiles + 8, 2 * half_tiles, 2 * half_tiles, 2 * wide_tiles, 2 * wide_tiles, 2 * half_tiles, 2 * half_tiles, 2 * wide_tiles)]
+
     def greet(sync):
         return [
-            remote(msg.at[sync], heard.at[sync, bn], ssem.at[sync, k], rsem.at[sync, k], target)
+            remote(msg.at[sync, lines[sync]], heard.at[sync, bn, lines[sync]], ssem.at[sync, k], rsem.at[sync, k], target)
             for k, target in enumerate(others)]
 
     def send(sync):
-        heard[sync, bn] = msg[sync]
+        heard[sync, bn, lines[sync], :] = msg[sync, lines[sync], :]
         for copy in greet(sync):
             copy.start()
 
     def receive(sync):
         for copy in greet(sync):
             copy.wait()
-        total = heard[sync, 0]
+        total = heard[sync, 0, lines[sync], :]
         for k in range(1, n_bn):
-            total = total + heard[sync, k]
+            total = total + heard[sync, k, lines[sync], :]
         return total
 
     def set_stat(slot, total, count, first_tile, tiles):
@@ -243,6 +248,8 @@
         spread = total[tiles : 2 * tiles] / count - mean * mean
         stat[slot, 0, 0:tiles, :] = mean
         stat[slot, 1, 0:tiles, :] = lax.rsqrt(spread + EPS)
+
+    def set_affine(slot, first_tile, tiles):
         for j in range(tiles):
             stat[slot, 2, j : j + 1, :] = aff_ref[2 * (first_tile + j) : 2 * (first_tile + j) + 1, :]
             stat[slot, 3, j : j + 1, :] = aff_ref[2 * (first_tile + j) + 1 : 2 * (first_tile + j) + 2, :]
@@ -280,11 +287,16 @@
         put_sums(sync, j, first, second, tiles)
 
     def set_back(slot, total, count, first_tile, tiles):
-        for j in range(tiles):
-            sums_ref[2 * (first_tile + j) : 2 * (first_tile + j) + 1, :] = total[tiles + j : tiles + j + 1]
-            sums_ref[2 * (first_tile + j) + 1 : 2 * (first_tile + j) + 2, :] = total[j : j + 1]
         stat[slot, 4, 0:tiles, :] = total[0:tiles] / count
         stat[slot, 5, 0:tiles, :] = total[tiles : 2 * tiles] / count
+        stat[slot, 6, 0:tiles, :] = total[tiles : 2 * tiles]
+        stat[slot, 7, 0:tiles, :] = total[0:tiles]
+
+    def put_affine(slot, first_tile, tiles):
+        for j in range(tiles):
+            for c in range(2):
+                at = 2 * (first_tile + j) + c
+                sums_ref[at : at + 1, :] = stat[slot, 6 + c, j : j + 1, :]
 
     def backward(slot, z, inner_ref, tiles, put):
         def body(j, cs):
@@ -437,6 +449,8 @@
                 phases[p, 0:LEAD, :] = jnp.zeros((LEAD, cin), F32)
                 tail = LEAD + pitch * grid
                 phases[p, tail:, :] = jnp.zeros((phases.shape[1] - tail, cin), F32)
+            for norm in norms:
+                set_affine(*norm)
             load_i.wait()
             for line in range(2 * grid):
                 slot = line % 2
@@ -675,6 +689,8 @@
                         forward_copy.start()
                 else:
                     advance(token, compute)
+            for norm in norms:
+                put_affine(*norm)
             for copy in own_e + [own_a, keep_e, keep_a, store_act]:
                 copy.wait()
 
@@ -856,7 +872,7 @@
         [pltpu.VMEM((n,) + shape, F32) for shape, n in shapes.items()],
         [pltpu.VMEM((n,) + shape, F32) for shape, n in finals.items()],
         pltpu.VMEM((rows + LEAD, width), F32), pltpu.VMEM((rows, half), F32),
-        pltpu.VMEM((rows, LANES), F32), pltpu.VMEM((4, 6, 8, LANES), F32),
+        pltpu.VMEM((rows, LANES), F32), pltpu.VMEM((4, 8, 8, LANES), F32),
         pltpu.VMEM((8, 3 * tiles, LANES), F32), pltpu.VMEM((8, n_bn, 3 * tiles, LANES), F32),
         pltpu.VMEM(aff.shape, F32), pltpu.VMEM((n_bits,) + aff.shape, F32),
         dma((8 + width // 256,)), dma((8, n_bn - 1)), dma((8, n_bn - 1)), dma((16,)), dma((16,)), dma((16,)),

time: 195 us -> 193 us (0.990)
  Pallas kernels: 193 us -> 190 us
    pallas_call x1, Pallas kernels: 185 us -> 183 us  [fused(): pl.pallas_call(functools.partial(fused_kernel, dims), out_shape=out, in_s...]
where the time goes in v4:
time: 193 us
  Pallas kernels  190 us (98%)
  between operations  2.13 us (1%)
    pallas_call x1, Pallas kernels, fused(): pl.pallas_call(functools.partial(fused_kernel, dims), out_shape=out, in_s...  183 us
    pallas_call x1, Pallas kernels, finish(): pl.pallas_call(functools.partial(finish_kernel, parts, len(arrays), tiles...  7.62 us

profile of v4, /device:TPU:0, one launch (start us, length us, event | category | flops | bytes accessed | tf_op | source)
XLA Modules:
  0.0 192.5 jit_solution(16637369078244392846)
XLA Ops:
  1.9 182.8 %section.1 = (f32[2888,128]{1,0:T(8,128)}, f32[5776,128]{1,0:T(8,128)}, f32[9,64,1024]{2,1,0:T(8,128)}, f32[9,64,512]{2,1,0:T(8,128)}, f32[128,1024]{1,0:T(8,128...) custom-call(s32[1]{0:T(128)S(6)} %copy.28.count_ref, ...), custom_call_target="tpu_custom_call" | custom-call | tf_op jit(solution)/shard_map/section/pallas_call | solution.py:881
  184.8 7.6 %finish.1 = (f32[2888,128]{1,0:T(8,128)}, f32[5776,128]{1,0:T(8,128)}, f32[9,64,1024]{2,1,0:T(8,128)}, f32[9,64,512]{2,1,0:T(8,128)}, f32[128,1024]{1,0:T(8,128)...) custom-call(f32[48,128]{1,0:T(8,128)} %get-tuple-element.29.sums_hbm, ...), custom_call_target="tpu_custom_call" | custom-call | tf_op jit(solution)/shard_map/finish/pallas_call | solution.py:930
